TPU v7x, 512 devices: a whole 4x8x8 slice. The times are simulated.
512 devices in a mesh: seq: 16 (over y, core), head: 32 (over x, z).
Axes of the slice: x: 4, y: 8, z: 8, core: 2. Of those that a mesh axis runs over, the one named last changes fastest.
Arguments:
- x_raw: bfloat16 [4096, 16384], P('seq', 'head'), may hold values from -10 to 10
- bc_raw: bfloat16 [4096, 4096], P('seq'), may hold values from -10 to 10
- z_raw: bfloat16 [4096, 16384], P('seq', 'head'), may hold values from -3000 to 3000
- x_kernel: float32 [4, 16384], P(None, 'head'), may hold values from -3 to 3
- bc_kernel: float32 [4, 4096], replicated, may hold values from -3 to 3
- x_offset: float32 [16384], P('head'), may hold values from -1.6 to -0.4
- bc_offset: float32 [4096], replicated, may hold values from -1.6 to -0.4
- dt_raw: float32 [4096, 256], P('seq', 'head'), may hold values from -1.5 to 9.5
- dt_bias: float32 [256], P('head'), may hold values from -7 to -2.5
- a_log: float32 [256], P('head'), may hold values from -5 to 3.5
- d_skip: float32 [256], P('head'), may hold values from 0.5 to 1.5
- norm_gain: float32 [16384], P('head'), may hold values from 0.25 to 1.75
- out_weight: bfloat16 [16384, 8192], P('head', 'seq'), may hold values from -0.09375 to 0.09375
Outputs:
- mixed: bfloat16 [4096, 8192], P('seq', 'head')
All inputs are finite; a program needn't handle non-finite values.
Results may differ from a plain program's by a relative error of at most 0.034.
Values may be sent and summed in bfloat16 or wider, within the bound.
A program may use at most 64 MiB of HBM per device.

v0:
```python
import jax
import jax.numpy as jnp
from jax import lax
from jax.sharding import PartitionSpec as P

P_SIZE = 64
N = 256
HPG = 32
SPAN = 256


norm_eps = 1e-05


def passed_along(block, axis, distance):
    devices = range(lax.axis_size(axis))
    route = [(i - distance, i) for i in devices if i - distance in devices]
    return lax.ppermute(block, axis, route)


def causal_conv(raw, prefix, kernel, offset):
    taps = kernel.shape[0]
    length = raw.shape[0]
    padded = jnp.concatenate([prefix.astype(jnp.float32), raw.astype(jnp.float32)], axis=0)
    running = jnp.zeros((length, raw.shape[1]), jnp.float32) + offset[None, :]
    for k in range(taps):
        running = running + kernel[k][None, :] * padded[k : k + length]
    return jax.nn.silu(running).astype(jnp.bfloat16)


def per_device(
    x_raw,
    bc_raw,
    z_raw,
    x_kernel,
    bc_kernel,
    x_offset,
    bc_offset,
    dt_raw,
    dt_bias,
    a_log,
    d_skip,
    norm_gain,
    out_weight,
):
    tok_rows, chan_width = x_raw.shape
    head_dev = dt_raw.shape[1]
    group_count = bc_raw.shape[1] // (2 * N)
    taps = x_kernel.shape[0]
    head_index = lax.axis_index("head")
    group_id = head_index * head_dev // HPG
    b_start = group_id * N
    c_start = (group_count + group_id) * N
    bc_own = jnp.concatenate(
        [
            lax.dynamic_slice_in_dim(bc_raw, b_start, N, 1),
            lax.dynamic_slice_in_dim(bc_raw, c_start, N, 1),
        ],
        axis=1,
    )
    kernel_own = jnp.concatenate(
        [
            lax.dynamic_slice_in_dim(bc_kernel, b_start, N, 1),
            lax.dynamic_slice_in_dim(bc_kernel, c_start, N, 1),
        ],
        axis=1,
    )
    offset_own = jnp.concatenate(
        [
            lax.dynamic_slice_in_dim(bc_offset, b_start, N, 0),
            lax.dynamic_slice_in_dim(bc_offset, c_start, N, 0),
        ],
        axis=0,
    )
    x_prior, bc_prior = passed_along(
        (x_raw[tok_rows - (taps - 1) :], bc_own[tok_rows - (taps - 1) :]), "seq", 1
    )
    x_conv = causal_conv(x_raw, x_prior, x_kernel, x_offset)
    bc_conv = causal_conv(bc_own, bc_prior, kernel_own, offset_own)
    span_count = tok_rows // SPAN
    step_size = jax.nn.softplus(dt_raw + dt_bias[None, :])
    a_rate = -jnp.exp(a_log)
    x_spans = x_conv.reshape(span_count, SPAN, head_dev, P_SIZE)
    b_spans = bc_conv[:, :N].reshape(span_count, SPAN, N)
    c_spans = bc_conv[:, N:].reshape(span_count, SPAN, N)
    dt_spans = step_size.reshape(span_count, SPAN, head_dev)
    cum_logs = jnp.cumsum(dt_spans * a_rate[None, None, :], axis=1)
    logs_heads = jnp.transpose(cum_logs, (0, 2, 1))
    positions = jnp.arange(SPAN)
    causal_mask = (positions[:, None] >= positions[None, :])[None, None]
    pair_gap = logs_heads[:, :, :, None] - logs_heads[:, :, None, :]
    decay_mask = jnp.where(causal_mask, jnp.exp(jnp.where(causal_mask, pair_gap, 0.0)), 0.0)
    inner_cb = jnp.einsum("ktn,ksn->kts", c_spans, b_spans, preferred_element_type=jnp.float32)
    dt_heads = jnp.transpose(dt_spans, (0, 2, 1))
    mixing = (decay_mask * inner_cb[:, None] * dt_heads[:, :, None, :]).astype(jnp.bfloat16)
    y_diag = jnp.einsum("khts,kshp->kthp", mixing, x_spans, preferred_element_type=jnp.float32)
    block_decay = cum_logs[:, -1, :]
    end_weight = jnp.exp(block_decay[:, None, :] - cum_logs) * dt_spans
    x_float = x_spans.astype(jnp.float32)
    input_weighted = (x_float * end_weight[..., None]).astype(jnp.bfloat16)
    local_state = jnp.einsum(
        "kthp,ktn->khpn", input_weighted, b_spans, preferred_element_type=jnp.float32
    )
    total_state = jnp.zeros((head_dev, P_SIZE, N), jnp.float32)
    k = 0
    total_state = jnp.exp(block_decay[k])[:, None, None] * total_state + local_state[k]
    total_log = block_decay[k]
    zero_state = jnp.zeros((head_dev, P_SIZE, N), jnp.float32)
    device_decay = jnp.exp(total_log)[:, None, None]

    def relay_step(step, carried):
        return passed_along(
            (device_decay * carried + total_state).astype(jnp.bfloat16), "seq", 1
        ).astype(jnp.float32)

    incoming = lax.fori_loop(0, lax.axis_size("seq") - 1, relay_step, zero_state)
    carried = incoming
    k = 0
    entering_list = [carried]
    carried = jnp.exp(block_decay[k])[:, None, None] * carried + local_state[k]
    entering = jnp.stack(entering_list, axis=0)
    y_off = jnp.einsum(
        "ktn,khpn->kthp", c_spans.astype(jnp.float32), entering, precision=lax.Precision.HIGHEST
    )
    y_off = y_off * jnp.exp(cum_logs)[..., None]
    y_all = (y_diag + y_off + d_skip[None, None, :, None] * x_float).reshape(tok_rows, chan_width)
    gated = y_all * jax.nn.silu(z_raw.astype(jnp.float32))
    own_squares = jnp.sum(gated * gated, axis=1)
    group_onehot = (jnp.arange(group_count) == group_id).astype(jnp.float32)
    group_table = lax.psum(own_squares[:, None] * group_onehot[None, :], "head")
    mean_square = jnp.sum(group_table * group_onehot[None, :], axis=1) / (HPG * P_SIZE)
    inv_rms = lax.rsqrt(mean_square + norm_eps)
    normed = (gated * inv_rms[:, None] * norm_gain[None, :]).astype(jnp.bfloat16)
    partial_value = jnp.dot(
        normed,
        lax.all_gather(out_weight, "seq", axis=1, tiled=True),
        preferred_element_type=jnp.float32,
    ).astype(jnp.bfloat16)
    summed = lax.psum(partial_value, "head").astype(jnp.float32)
    local_columns = summed.shape[1] // lax.axis_size("head")
    result = lax.dynamic_slice_in_dim(summed, head_index * local_columns, local_columns, 1)
    return result.astype(jnp.bfloat16)


def solution(mesh):
    return jax.shard_map(
        per_device,
        mesh=mesh,
        in_specs=(
            P("seq", "head"),
            P("seq", None),
            P("seq", "head"),
            P(None, "head"),
            P(),
            P("head"),
            P(),
            P("seq", "head"),
            P("head"),
            P("head"),
            P("head"),
            P("head"),
            P("head", "seq"),
        ),
        out_specs=P("seq", "head"),
        check_vma=False,
    )
```

profile of v0, /device:TPU:8, one launch (start us, length us, event | category | flops | bytes accessed | tf_op | source)
XLA Modules:
  0.0 444.3 jit_solution(4355739217931496939)
XLA Ops:
  6.6 0.7 all-gather.2.cloned.1.call-update
  7.3 0.7 slice.64
  8.0 1.9 collective-permute-start.1
  10.0 1.0 constant_dynamic-slice_fusion.1
  11.0 3.6 collective-permute-start.2
  14.6 0.7 exponential_negate_fusion
  15.2 0.8 fusion.50
  16.0 0.6 reduce-window.6
  16.8 0.8 fusion.53
  17.9 0.7 constant_dynamic-slice_fusion.3
  19.3 0.4 multiply_convert_fusion.3
  20.7 137.5 %while.11 = (s32[]{:T(128)}, f32[8,64,256]{2,1,0:T(8,128)S(1)}, f32[8,1,1]{0,2,1:T(1,128)S(1)}, f32[8,64,256]{2,1,0:T(8,128)S(1)}, s32[]{:T(128)}, /*index=5*/s32[]{:T(128)}) while((s32[]{:T(128)}, f32[8,64,256]{2,1,0:T(8,128)S(1)}, f32[8,1,1]{0,2,1:T(1,128)S(1)}, f32[8,64,256]{2,1,0:T(8,128)S(1)}, s32[]{:T(128)}, ...), condition=%wide.region_3.4_spmd.clone, body=%wide.region_2.3_spmd.clone.sunk | while | flops 655363 | bytes 3145879 | solution.py:116
  20.9 1.9 collective-permute-start
  22.8 5.8 %collective-permute-done = bf16[8,64,256]{2,1,0:T(8,128)(2,1)S(1)} collective-permute-done((bf16[8,64,256]{2,1,0:T(8,128)(2,1)S(1)}, bf16[8,64,256]{2,1,0:T(8,128)(2,1)S(1)}, u32[]{:S(2)}, u32[]{:S(2)}) %collective-permute-start) | collective-permute-done | bytes 262176 | tf_op jit(solution)/shard_map/while/body/eval_jaxpr/ppermute | solution.py:18
  28.7 1.9 collective-permute-start
  30.7 11.0 %collective-permute-done = bf16[8,64,256]{2,1,0:T(8,128)(2,1)S(1)} collective-permute-done((bf16[8,64,256]{2,1,0:T(8,128)(2,1)S(1)}, bf16[8,64,256]{2,1,0:T(8,128)(2,1)S(1)}, u32[]{:S(2)}, u32[]{:S(2)}) %collective-permute-start) | collective-permute-done | bytes 262176 | tf_op jit(solution)/shard_map/while/body/eval_jaxpr/ppermute | solution.py:18
  41.9 1.9 collective-permute-start
  43.8 11.4 %collective-permute-done = bf16[8,64,256]{2,1,0:T(8,128)(2,1)S(1)} collective-permute-done((bf16[8,64,256]{2,1,0:T(8,128)(2,1)S(1)}, bf16[8,64,256]{2,1,0:T(8,128)(2,1)S(1)}, u32[]{:S(2)}, u32[]{:S(2)}) %collective-permute-start) | collective-permute-done | bytes 262176 | tf_op jit(solution)/shard_map/while/body/eval_jaxpr/ppermute | solution.py:18
  55.4 1.9 collective-permute-start
  57.3 11.4 %collective-permute-done = bf16[8,64,256]{2,1,0:T(8,128)(2,1)S(1)} collective-permute-done((bf16[8,64,256]{2,1,0:T(8,128)(2,1)S(1)}, bf16[8,64,256]{2,1,0:T(8,128)(2,1)S(1)}, u32[]{:S(2)}, u32[]{:S(2)}) %collective-permute-start) | collective-permute-done | bytes 262176 | tf_op jit(solution)/shard_map/while/body/eval_jaxpr/ppermute | solution.py:18
  68.9 1.9 collective-permute-start
  70.8 8.5 %collective-permute-done = bf16[8,64,256]{2,1,0:T(8,128)(2,1)S(1)} collective-permute-done((bf16[8,64,256]{2,1,0:T(8,128)(2,1)S(1)}, bf16[8,64,256]{2,1,0:T(8,128)(2,1)S(1)}, u32[]{:S(2)}, u32[]{:S(2)}) %collective-permute-start) | collective-permute-done | bytes 262176 | tf_op jit(solution)/shard_map/while/body/eval_jaxpr/ppermute | solution.py:18
  79.5 1.9 collective-permute-start
  81.4 5.8 %collective-permute-done = bf16[8,64,256]{2,1,0:T(8,128)(2,1)S(1)} collective-permute-done((bf16[8,64,256]{2,1,0:T(8,128)(2,1)S(1)}, bf16[8,64,256]{2,1,0:T(8,128)(2,1)S(1)}, u32[]{:S(2)}, u32[]{:S(2)}) %collective-permute-start) | collective-permute-done | bytes 262176 | tf_op jit(solution)/shard_map/while/body/eval_jaxpr/ppermute | solution.py:18
  87.4 1.9 collective-permute-start
  89.3 5.8 %collective-permute-done = bf16[8,64,256]{2,1,0:T(8,128)(2,1)S(1)} collective-permute-done((bf16[8,64,256]{2,1,0:T(8,128)(2,1)S(1)}, bf16[8,64,256]{2,1,0:T(8,128)(2,1)S(1)}, u32[]{:S(2)}, u32[]{:S(2)}) %collective-permute-start) | collective-permute-done | bytes 262176 | tf_op jit(solution)/shard_map/while/body/eval_jaxpr/ppermute | solution.py:18
  95.3 1.9 collective-permute-start
  97.2 5.8 %collective-permute-done = bf16[8,64,256]{2,1,0:T(8,128)(2,1)S(1)} collective-permute-done((bf16[8,64,256]{2,1,0:T(8,128)(2,1)S(1)}, bf16[8,64,256]{2,1,0:T(8,128)(2,1)S(1)}, u32[]{:S(2)}, u32[]{:S(2)}) %collective-permute-start) | collective-permute-done | bytes 262176 | tf_op jit(solution)/shard_map/while/body/eval_jaxpr/ppermute | solution.py:18
  103.2 1.9 collective-permute-start
  105.1 5.8 %collective-permute-done = bf16[8,64,256]{2,1,0:T(8,128)(2,1)S(1)} collective-permute-done((bf16[8,64,256]{2,1,0:T(8,128)(2,1)S(1)}, bf16[8,64,256]{2,1,0:T(8,128)(2,1)S(1)}, u32[]{:S(2)}, u32[]{:S(2)}) %collective-permute-start) | collective-permute-done | bytes 262176 | tf_op jit(solution)/shard_map/while/body/eval_jaxpr/ppermute | solution.py:18
  111.1 1.9 collective-permute-start
  113.0 5.8 %collective-permute-done = bf16[8,64,256]{2,1,0:T(8,128)(2,1)S(1)} collective-permute-done((bf16[8,64,256]{2,1,0:T(8,128)(2,1)S(1)}, bf16[8,64,256]{2,1,0:T(8,128)(2,1)S(1)}, u32[]{:S(2)}, u32[]{:S(2)}) %collective-permute-start) | collective-permute-done | bytes 262176 | tf_op jit(solution)/shard_map/while/body/eval_jaxpr/ppermute | solution.py:18
  118.9 1.9 collective-permute-start
  120.9 5.8 %collective-permute-done = bf16[8,64,256]{2,1,0:T(8,128)(2,1)S(1)} collective-permute-done((bf16[8,64,256]{2,1,0:T(8,128)(2,1)S(1)}, bf16[8,64,256]{2,1,0:T(8,128)(2,1)S(1)}, u32[]{:S(2)}, u32[]{:S(2)}) %collective-permute-start) | collective-permute-done | bytes 262176 | tf_op jit(solution)/shard_map/while/body/eval_jaxpr/ppermute | solution.py:18
  126.8 1.9 collective-permute-start
  128.8 5.8 %collective-permute-done = bf16[8,64,256]{2,1,0:T(8,128)(2,1)S(1)} collective-permute-done((bf16[8,64,256]{2,1,0:T(8,128)(2,1)S(1)}, bf16[8,64,256]{2,1,0:T(8,128)(2,1)S(1)}, u32[]{:S(2)}, u32[]{:S(2)}) %collective-permute-start) | collective-permute-done | bytes 262176 | tf_op jit(solution)/shard_map/while/body/eval_jaxpr/ppermute | solution.py:18
  134.7 1.9 collective-permute-start
  136.6 5.8 %collective-permute-done = bf16[8,64,256]{2,1,0:T(8,128)(2,1)S(1)} collective-permute-done((bf16[8,64,256]{2,1,0:T(8,128)(2,1)S(1)}, bf16[8,64,256]{2,1,0:T(8,128)(2,1)S(1)}, u32[]{:S(2)}, u32[]{:S(2)}) %collective-permute-start) | collective-permute-done | bytes 262176 | tf_op jit(solution)/shard_map/while/body/eval_jaxpr/ppermute | solution.py:18
  142.6 1.9 collective-permute-start
  144.5 5.8 %collective-permute-done = bf16[8,64,256]{2,1,0:T(8,128)(2,1)S(1)} collective-permute-done((bf16[8,64,256]{2,1,0:T(8,128)(2,1)S(1)}, bf16[8,64,256]{2,1,0:T(8,128)(2,1)S(1)}, u32[]{:S(2)}, u32[]{:S(2)}) %collective-permute-start) | collective-permute-done | bytes 262176 | tf_op jit(solution)/shard_map/while/body/eval_jaxpr/ppermute | solution.py:18
  150.5 1.9 collective-permute-start
  152.4 5.8 %collective-permute-done = bf16[8,64,256]{2,1,0:T(8,128)(2,1)S(1)} collective-permute-done((bf16[8,64,256]{2,1,0:T(8,128)(2,1)S(1)}, bf16[8,64,256]{2,1,0:T(8,128)(2,1)S(1)}, u32[]{:S(2)}, u32[]{:S(2)}) %collective-permute-start) | collective-permute-done | bytes 262176 | tf_op jit(solution)/shard_map/while/body/eval_jaxpr/ppermute | solution.py:18
  158.2 0.4 fusion.4
  158.9 0.9 fusion.3
  160.3 84.8 %psum.14 = f32[256,8]{0,1:T(8,128)S(1)} all-reduce(f32[256,8]{0,1:T(8,128)S(1)} %broadcast_multiply_fusion), channel_id=1, replica_groups=mesh['seq'=16,'head'=32] {'head'}, use_global_device_ids=true, to_apply=%region_5.6 | all-reduce | flops 2048 | bytes 16384 | tf_op jit(solution)/shard_map/psum | solution.py:130
  245.2 7.8 %convolution_convert_fusion = bf16[256,8192]{1,0:T(8,128)(2,1)} fusion(bf16[512,8192]{1,0:T(8,128)(2,1)} %all-gather.2.cloned.1.call-done, f32[512]{0:T(512)S(1)} %copy-done.6, f32[256]{0:T(256)S(1)} %add_rsqrt_fusion, f32[256,512]{1,0:T(8,128)S(1)} %copy.27, bf16[256,512]{1,0:T(8,128)(2,1)S(1)} %copy-done.1), kind=kOutput, calls=%fused_computation.3 | convolution fusion | flops 2150760448 | bytes 13372416 | tf_op jit(solution)/shard_map/dot_general | solution.py:134
  253.0 182.8 %all-reduce.2.cloned.1.call-done = bf16[256,8192]{1,0:T(8,128)(2,1)} async-done(((bf16[256,8192]{1,0:T(8,128)(2,1)}), bf16[256,8192]{1,0:T(8,128)(2,1)}) %all-reduce.2.cloned.1.call-update) | async-done | bytes 4194320 | tf_op jit(solution)/shard_map/psum | solution.py:139
  435.9 1.6 convert_convert_fusion
  (84 shorter events, 5.5 us)
Async XLA Ops:
  6.5 12.4 %copy-start = (bf16[256,512]{1,0:T(8,128)(2,1)S(1)}, bf16[256,512]{1,0:T(8,128)(2,1)}, u32[]{:S(2)}) copy-start(bf16[256,512]{1,0:T(8,128)(2,1)} %param.15) | copy-start | bytes 786436
  6.5 12.3 %copy-start.5 = (f32[8]{0:T(128)S(1)}, f32[8]{0:T(128)}, u32[]{:S(2)}) copy-start(f32[8]{0:T(128)} %param.23) | copy-start | bytes 100
  6.5 12.3 %copy-start.2 = (f32[256,8]{0,1:T(8,128)S(1)}, f32[256,8]{0,1:T(8,128)}, u32[]{:S(2)}) copy-start(f32[256,8]{0,1:T(8,128)} %param.22) | copy-start | bytes 24580
  6.5 12.2 %copy-start.3 = (f32[4,512]{1,0:T(4,128)S(1)}, f32[4,512]{1,0:T(4,128)}, u32[]{:S(2)}) copy-start(f32[4,512]{1,0:T(4,128)} %param.18) | copy-start | bytes 24580
  6.5 238.6 %all-gather.2.cloned.1.call-start = ((), (), s32[]{:S(2)}) async-start(), calls=%async_computation | async-start | bytes 8912896 | tf_op jit(solution)/shard_map/all_gather | solution.py:136
  7.3 428.6 %all-reduce.2.cloned.1.call-start = ((), (), s32[]{:S(2)}) async-start(), calls=%async_computation.1 | async-start | bytes 8388608 | tf_op jit(solution)/shard_map/psum | solution.py:139
  8.0 11.2 %collective-permute-start.1 = (bf16[3,512]{1,0:T(4,128)(2,1)S(1)}, bf16[3,512]{1,0:T(4,128)(2,1)S(1)}, u32[]{:S(2)}, u32[]{:S(2)}) collective-permute-start(bf16[3,512]{1,0:T(4,128)(2,1)S(1)} %slice.64), channel_id=1, source_target_pairs={{0,32},{32,64},{64,96},{96,128},{128,160},{160,192},{192,224},{224... | collective-permute-start | bytes 9224 | tf_op jit(solution)/shard_map/ppermute | solution.py:18
  10.0 9.3 %copy-start.4 = (f32[512]{0:T(512)S(1)}, f32[512]{0:T(512)}, u32[]{:S(2)}) copy-start(f32[512]{0:T(512)} %param.20) | copy-start | bytes 6148
  11.0 9.1 %collective-permute-start.2 = (bf16[3,512]{1,0:T(4,128)(2,1)S(1)}, bf16[3,512]{1,0:T(4,128)(2,1)S(1)}, u32[]{:S(2)}, u32[]{:S(2)}) collective-permute-start(bf16[3,512]{1,0:T(4,128)(2,1)S(1)} %fusion.45), channel_id=1, source_target_pairs={{0,32},{32,64},{64,96},{96,128},{128,160},{160,192},{192,224},{224... | collective-permute-start | bytes 9224 | tf_op jit(solution)/shard_map/ppermute | solution.py:18
  20.7 138.2 %copy-start.7 = (f32[8]{0:T(128)S(1)}, f32[8]{0:T(128)}, u32[]{:S(2)}) copy-start(f32[8]{0:T(128)} %param.25) | copy-start | bytes 100
  20.9 7.7 %collective-permute-start = (bf16[8,64,256]{2,1,0:T(8,128)(2,1)S(1)}, bf16[8,64,256]{2,1,0:T(8,128)(2,1)S(1)}, u32[]{:S(2)}, u32[]{:S(2)}) collective-permute-start(bf16[8,64,256]{2,1,0:T(8,128)(2,1)S(1)} %fusion.60), channel_id=1, source_target_pairs={{0,32},{32,64},{64,96},{96,128},{128,160},{160,192},{192,224},{224... | collective-permute-start | bytes 786440 | tf_op jit(solution)/shard_map/while/body/eval_jaxpr/ppermute | solution.py:18
  28.7 13.0 %collective-permute-start = (bf16[8,64,256]{2,1,0:T(8,128)(2,1)S(1)}, bf16[8,64,256]{2,1,0:T(8,128)(2,1)S(1)}, u32[]{:S(2)}, u32[]{:S(2)}) collective-permute-start(bf16[8,64,256]{2,1,0:T(8,128)(2,1)S(1)} %fusion.60), channel_id=1, source_target_pairs={{0,32},{32,64},{64,96},{96,128},{128,160},{160,192},{192,224},{224... | collective-permute-start | bytes 786440 | tf_op jit(solution)/shard_map/while/body/eval_jaxpr/ppermute | solution.py:18
  41.9 13.3 %collective-permute-start = (bf16[8,64,256]{2,1,0:T(8,128)(2,1)S(1)}, bf16[8,64,256]{2,1,0:T(8,128)(2,1)S(1)}, u32[]{:S(2)}, u32[]{:S(2)}) collective-permute-start(bf16[8,64,256]{2,1,0:T(8,128)(2,1)S(1)} %fusion.60), channel_id=1, source_target_pairs={{0,32},{32,64},{64,96},{96,128},{128,160},{160,192},{192,224},{224... | collective-permute-start | bytes 786440 | tf_op jit(solution)/shard_map/while/body/eval_jaxpr/ppermute | solution.py:18
  55.4 13.3 %collective-permute-start = (bf16[8,64,256]{2,1,0:T(8,128)(2,1)S(1)}, bf16[8,64,256]{2,1,0:T(8,128)(2,1)S(1)}, u32[]{:S(2)}, u32[]{:S(2)}) collective-permute-start(bf16[8,64,256]{2,1,0:T(8,128)(2,1)S(1)} %fusion.60), channel_id=1, source_target_pairs={{0,32},{32,64},{64,96},{96,128},{128,160},{160,192},{192,224},{224... | collective-permute-start | bytes 786440 | tf_op jit(solution)/shard_map/while/body/eval_jaxpr/ppermute | solution.py:18
  68.9 10.5 %collective-permute-start = (bf16[8,64,256]{2,1,0:T(8,128)(2,1)S(1)}, bf16[8,64,256]{2,1,0:T(8,128)(2,1)S(1)}, u32[]{:S(2)}, u32[]{:S(2)}) collective-permute-start(bf16[8,64,256]{2,1,0:T(8,128)(2,1)S(1)} %fusion.60), channel_id=1, source_target_pairs={{0,32},{32,64},{64,96},{96,128},{128,160},{160,192},{192,224},{224... | collective-permute-start | bytes 786440 | tf_op jit(solution)/shard_map/while/body/eval_jaxpr/ppermute | solution.py:18
  79.5 7.7 %collective-permute-start = (bf16[8,64,256]{2,1,0:T(8,128)(2,1)S(1)}, bf16[8,64,256]{2,1,0:T(8,128)(2,1)S(1)}, u32[]{:S(2)}, u32[]{:S(2)}) collective-permute-start(bf16[8,64,256]{2,1,0:T(8,128)(2,1)S(1)} %fusion.60), channel_id=1, source_target_pairs={{0,32},{32,64},{64,96},{96,128},{128,160},{160,192},{192,224},{224... | collective-permute-start | bytes 786440 | tf_op jit(solution)/shard_map/while/body/eval_jaxpr/ppermute | solution.py:18
  87.4 7.7 %collective-permute-start = (bf16[8,64,256]{2,1,0:T(8,128)(2,1)S(1)}, bf16[8,64,256]{2,1,0:T(8,128)(2,1)S(1)}, u32[]{:S(2)}, u32[]{:S(2)}) collective-permute-start(bf16[8,64,256]{2,1,0:T(8,128)(2,1)S(1)} %fusion.60), channel_id=1, source_target_pairs={{0,32},{32,64},{64,96},{96,128},{128,160},{160,192},{192,224},{224... | collective-permute-start | bytes 786440 | tf_op jit(solution)/shard_map/while/body/eval_jaxpr/ppermute | solution.py:18
  95.3 7.7 %collective-permute-start = (bf16[8,64,256]{2,1,0:T(8,128)(2,1)S(1)}, bf16[8,64,256]{2,1,0:T(8,128)(2,1)S(1)}, u32[]{:S(2)}, u32[]{:S(2)}) collective-permute-start(bf16[8,64,256]{2,1,0:T(8,128)(2,1)S(1)} %fusion.60), channel_id=1, source_target_pairs={{0,32},{32,64},{64,96},{96,128},{128,160},{160,192},{192,224},{224... | collective-permute-start | bytes 786440 | tf_op jit(solution)/shard_map/while/body/eval_jaxpr/ppermute | solution.py:18
  103.2 7.7 %collective-permute-start = (bf16[8,64,256]{2,1,0:T(8,128)(2,1)S(1)}, bf16[8,64,256]{2,1,0:T(8,128)(2,1)S(1)}, u32[]{:S(2)}, u32[]{:S(2)}) collective-permute-start(bf16[8,64,256]{2,1,0:T(8,128)(2,1)S(1)} %fusion.60), channel_id=1, source_target_pairs={{0,32},{32,64},{64,96},{96,128},{128,160},{160,192},{192,224},{224... | collective-permute-start | bytes 786440 | tf_op jit(solution)/shard_map/while/body/eval_jaxpr/ppermute | solution.py:18
  111.1 7.7 %collective-permute-start = (bf16[8,64,256]{2,1,0:T(8,128)(2,1)S(1)}, bf16[8,64,256]{2,1,0:T(8,128)(2,1)S(1)}, u32[]{:S(2)}, u32[]{:S(2)}) collective-permute-start(bf16[8,64,256]{2,1,0:T(8,128)(2,1)S(1)} %fusion.60), channel_id=1, source_target_pairs={{0,32},{32,64},{64,96},{96,128},{128,160},{160,192},{192,224},{224... | collective-permute-start | bytes 786440 | tf_op jit(solution)/shard_map/while/body/eval_jaxpr/ppermute | solution.py:18
  118.9 7.7 %collective-permute-start = (bf16[8,64,256]{2,1,0:T(8,128)(2,1)S(1)}, bf16[8,64,256]{2,1,0:T(8,128)(2,1)S(1)}, u32[]{:S(2)}, u32[]{:S(2)}) collective-permute-start(bf16[8,64,256]{2,1,0:T(8,128)(2,1)S(1)} %fusion.60), channel_id=1, source_target_pairs={{0,32},{32,64},{64,96},{96,128},{128,160},{160,192},{192,224},{224... | collective-permute-start | bytes 786440 | tf_op jit(solution)/shard_map/while/body/eval_jaxpr/ppermute | solution.py:18
  126.8 7.7 %collective-permute-start = (bf16[8,64,256]{2,1,0:T(8,128)(2,1)S(1)}, bf16[8,64,256]{2,1,0:T(8,128)(2,1)S(1)}, u32[]{:S(2)}, u32[]{:S(2)}) collective-permute-start(bf16[8,64,256]{2,1,0:T(8,128)(2,1)S(1)} %fusion.60), channel_id=1, source_target_pairs={{0,32},{32,64},{64,96},{96,128},{128,160},{160,192},{192,224},{224... | collective-permute-start | bytes 786440 | tf_op jit(solution)/shard_map/while/body/eval_jaxpr/ppermute | solution.py:18
  134.7 7.7 %collective-permute-start = (bf16[8,64,256]{2,1,0:T(8,128)(2,1)S(1)}, bf16[8,64,256]{2,1,0:T(8,128)(2,1)S(1)}, u32[]{:S(2)}, u32[]{:S(2)}) collective-permute-start(bf16[8,64,256]{2,1,0:T(8,128)(2,1)S(1)} %fusion.60), channel_id=1, source_target_pairs={{0,32},{32,64},{64,96},{96,128},{128,160},{160,192},{192,224},{224... | collective-permute-start | bytes 786440 | tf_op jit(solution)/shard_map/while/body/eval_jaxpr/ppermute | solution.py:18
  142.6 7.7 %collective-permute-start = (bf16[8,64,256]{2,1,0:T(8,128)(2,1)S(1)}, bf16[8,64,256]{2,1,0:T(8,128)(2,1)S(1)}, u32[]{:S(2)}, u32[]{:S(2)}) collective-permute-start(bf16[8,64,256]{2,1,0:T(8,128)(2,1)S(1)} %fusion.60), channel_id=1, source_target_pairs={{0,32},{32,64},{64,96},{96,128},{128,160},{160,192},{192,224},{224... | collective-permute-start | bytes 786440 | tf_op jit(solution)/shard_map/while/body/eval_jaxpr/ppermute | solution.py:18
  150.5 7.7 %collective-permute-start = (bf16[8,64,256]{2,1,0:T(8,128)(2,1)S(1)}, bf16[8,64,256]{2,1,0:T(8,128)(2,1)S(1)}, u32[]{:S(2)}, u32[]{:S(2)}) collective-permute-start(bf16[8,64,256]{2,1,0:T(8,128)(2,1)S(1)} %fusion.60), channel_id=1, source_target_pairs={{0,32},{32,64},{64,96},{96,128},{128,160},{160,192},{192,224},{224... | collective-permute-start | bytes 786440 | tf_op jit(solution)/shard_map/while/body/eval_jaxpr/ppermute | solution.py:18
  158.9 1.1 copy-start.1
  158.9 86.3 %copy-start.6 = (f32[512]{0:T(512)S(1)}, f32[512]{0:T(512)}, u32[]{:S(2)}) copy-start(f32[512]{0:T(512)} %param.26) | copy-start | bytes 6148
Sparse Core Ops, SparseCore 0:
  9.5 70.3 all-gather.1
  253.1 182.6 all-reduce.1
where the time goes:
time: 445 us; the launch traced here: 444 us
  waiting for transfers between devices  289 us (65%)
  blocking collectives  84.8 us (19%)
  starting transfers between devices  34.4 us (8%)
  between operations  13.8 us (3%)
  matrix products  9.52 us (2%)
  other arithmetic  7.69 us (2%)
    psum x1, waiting for transfers between devices, per_device(): summed = lax.psum(partial_value, 'head').astype(jnp.float32)  183 us
    ppermute x17, waiting for transfers between devices, passed_along(): return lax.ppermute(block, axis, route)  106 us
    psum x1, blocking collectives, per_device(): group_table = lax.psum(own_squares[:, None] * group_onehot[None, :], 'head')  84.8 us
    ppermute x17, starting transfers between devices, passed_along(): return lax.ppermute(block, axis, route)  34.3 us
  transfers between devices with their start and end apart: 19, of which 16 were waited for; matrix products, arithmetic and copies ran while one was open for 3% of the time, Pallas kernels for 0%

commit v1 on v0

v1 whole, which is shorter than its diff:
```python
import jax
import jax.numpy as jnp
from jax import lax
from jax.experimental import pallas as pl
from jax.experimental.pallas import tpu as pltpu
from jax.sharding import PartitionSpec as P

P_SIZE = 64
N = 256
TOK = 256
CH = 512
HEADS_DEV = 8
NY, NX, NZ = 8, 4, 8
SLOTS = 8
norm_eps = 1e-05
MESH = pl.DeviceIdType.MESH
HI = lax.Precision.HIGHEST
f32 = jnp.float32
bf16 = jnp.bfloat16


def dot(a, b, dims, precision=None):
    return lax.dot_general(a, b, (dims, ((), ())), precision=precision, preferred_element_type=f32)


def kernel(
    x_hbm,
    bc_hbm,
    z_hbm,
    xk_ref,
    bck_ref,
    xo_ref,
    bco_ref,
    dt_ref,
    dtb_ref,
    alog_ref,
    dsk_ref,
    gain_ref,
    w_hbm,
    o_ref,
    xbc,
    zb,
    wb,
    load_sem,
    halo,
    raw,
    conv,
    cum,
    dts,
    rows,
    ybase,
    state,
    statebf,
    sibstate,
    dec,
    decall,
    total,
    gath,
    entout,
    entchip,
    entsend,
    ent,
    sq,
    slot_in,
    part,
    xlong,
    xshort,
    strip,
    zin,
    fin,
    out,
    scan_send,
    scan_recv,
    y_send,
    y_recv,
    c_send,
    c_recv,
    x_send,
    x_recv,
    z_send,
    z_recv,
    f_send,
    f_recv,
):
    seq = lax.axis_index("seq")
    head = lax.axis_index("head")
    Y, C = seq // 2, seq % 2
    X, Z = head // NZ, head % NZ
    group = head // 4
    other = 1 - C

    def at(y, c, x, z):
        return (y * 2 + c, x * NZ + z)

    sibling = at(Y, other, X, Z)
    y_next, y_prev = lax.rem(Y + 1, NY), lax.rem(Y + NY - 1, NY)
    after = (lax.rem(seq + 1, 16), head)
    before = (lax.rem(seq + 15, 16), head)
    cross = at(lax.rem(Y + NY - 1 + 2 * C, NY), other, X, Z)
    sigma = 1 - 2 * C
    x_fwd = at(Y, C, lax.rem(X + NX + sigma, NX), Z)
    x_back = at(Y, C, lax.rem(X + NX - sigma, NX), Z)

    def y_at(k):
        return at(lax.rem(Y + k, NY), C, X, Z)

    def z_at(k):
        return at(Y, C, X, lax.rem(Z + k, NZ))

    owner_c = X // 2
    owner_x = Y // 2
    owner_z = 4 * lax.rem(Y, 2) + 2 * C

    def same(a, b):
        return jnp.logical_and(a[0] == b[0], a[1] == b[1])

    me = (seq, head)

    barrier = pltpu.get_barrier_semaphore()

    def greet(device):
        pl.semaphore_signal(barrier, inc=1, device_id=device, device_id_type=MESH)

    greet(sibling)
    greet(cross)
    for k in range(1, NY):
        greet(y_at(k))
    for k in range(1, NZ):
        greet(z_at(k))
    greet(x_fwd)
    greet(x_back)
    src_y = 2 * X + Z // 4
    src_c = lax.rem(Z // 2, 2)
    for dx in range(2):

        def greet_source(z, carry, dx=dx):
            device = at(src_y, src_c, 2 * C + dx, z)

            @pl.when(jnp.logical_not(same(device, me)))
            def _():
                greet(device)

            return carry

        lax.fori_loop(0, NZ, greet_source, 0)
    stays = jnp.logical_and(
        jnp.logical_and(owner_x == X, owner_c == C), Z // 2 == owner_z // 2
    ).astype(jnp.int32)

    def load(i, src, dst):
        copy = pltpu.make_async_copy(src, dst, load_sem.at[i])
        copy.start()
        return copy

    b_start = pl.multiple_of(group * N, N)
    c_start = pl.multiple_of(8 * N + group * N, N)
    loads = [
        load(0, x_hbm, xbc.at[:, pl.ds(0, CH)]),
        load(1, bc_hbm.at[:, pl.ds(b_start, N)], xbc.at[:, pl.ds(CH, N)]),
        load(2, bc_hbm.at[:, pl.ds(c_start, N)], xbc.at[:, pl.ds(CH + N, N)]),
    ]
    z_load = load(3, z_hbm, zb)
    w_load = load(4, w_hbm, wb)

    pos_t = lax.broadcasted_iota(jnp.int32, (TOK, TOK), 0)
    pos_s = lax.broadcasted_iota(jnp.int32, (TOK, TOK), 1)
    causal = pos_t >= pos_s
    step_in = dt_ref[...] + dtb_ref[...]
    step = jnp.maximum(step_in, 0.0) + jnp.log1p(jnp.exp(-jnp.abs(step_in)))
    log_step = step * -jnp.exp(alog_ref[...])
    cum_cols = dot(causal.astype(f32), log_step, ((1,), (0,)), HI)
    cum[...] = cum_cols
    dts[...] = step
    eye = (pos_t == pos_s).astype(f32)
    rows[0:8, :] = dot(cum_cols, eye, ((0,), (0,)), HI)
    rows[8:16, :] = dot(step, eye, ((0,), (0,)), HI)
    last_cols = cum_cols[TOK - 1 : TOK, :]
    dec[0] = jnp.broadcast_to(jnp.exp(rows[0:8, TOK - 1 : TOK]), (8, TOK))
    spread = (
        lax.broadcasted_iota(jnp.int32, (HEADS_DEV, CH), 1) // P_SIZE
        == lax.broadcasted_iota(jnp.int32, (HEADS_DEV, CH), 0)
    ).astype(f32)
    end_weight = dot(jnp.exp(last_cols - cum_cols) * step, spread, ((1,), (0,)), HI)

    for copy in loads:
        copy.wait()
    pl.semaphore_wait(barrier, 2 + (NY - 1) + (NZ - 1) + 2 + 16 - stays)

    def remote(src, dst, send, recv, device):
        return pltpu.make_async_remote_copy(
            src_ref=src, dst_ref=dst, send_sem=send, recv_sem=recv, device_id=device, device_id_type=MESH
        )

    def arrived(ref, sem):
        pltpu.make_async_copy(ref, ref, sem).wait()

    halo_copy = remote(xbc.at[pl.ds(TOK - 16, 16)], halo, scan_send.at[0], scan_recv.at[0], after)
    halo_copy.start()
    dec_copy = remote(dec.at[0], dec.at[1], scan_send.at[1], scan_recv.at[1], sibling)
    dec_copy.start()

    def convolve(first, count):
        for j in range(8):
            cols = slice(j * 128, (j + 1) * 128)
            if j < 4:
                taps = [xk_ref[k : k + 1, cols] for k in range(4)]
                offset = xo_ref[:, cols]
            else:
                start = (b_start if j < 6 else c_start) + (j % 2) * 128
                lanes = pl.ds(pl.multiple_of(start, 128), 128)
                taps = [bck_ref[k : k + 1, lanes] for k in range(4)]
                offset = bco_ref[:, lanes]
            acc = jnp.broadcast_to(offset, (count, 128))
            for k in range(4):
                acc = acc + taps[k] * raw[5 + k + first : 5 + k + first + count, cols]
            conv[first : first + count, cols] = (acc / (1.0 + jnp.exp(-acc))).astype(bf16)

    raw[8 : 8 + TOK, :] = xbc[...].astype(f32)
    convolve(16, TOK - 16)
    halo_copy.wait()
    not_first = (seq > 0).astype(f32)
    raw[0:8, :] = halo[...].astype(f32)[8:16, :] * not_first
    convolve(0, 16)

    dec_copy.wait()
    dec[2] = dec[0] * dec[1]
    decall[Y] = dec[2]
    dec_copies = []
    for k in range(1, NY):
        copy = remote(dec.at[2], decall.at[Y], scan_send.at[1 + k], scan_recv.at[2], y_at(k))
        copy.start()
        dec_copies.append(copy)

    x_conv = conv[:, 0:CH].astype(f32)
    weighted = (x_conv * end_weight).astype(bf16)
    own_state = dot(weighted, conv[:, CH : CH + N], ((0,), (0,)))
    state[...] = own_state
    statebf[...] = own_state.astype(bf16)
    sib_rows = pl.ds(pl.multiple_of(other * 256, 256), 256)
    own_rows = pl.ds(pl.multiple_of(C * 256, 256), 256)
    a_copy = remote(statebf.at[sib_rows], sibstate, scan_send.at[9], scan_recv.at[3], sibling)
    a_copy.start()

    b_conv = conv[:, CH : CH + N]
    c_conv = conv[:, CH + N : CH + 2 * N]
    inner = dot(c_conv, b_conv, ((1,), (1,)))

    def diagonal(h):
        gap = cum[:, h : h + 1] - rows[h : h + 1, :]
        mixing = jnp.exp(jnp.where(causal, gap, -jnp.inf)) * inner * rows[8 + h : 9 + h, :]
        lanes = slice(h * P_SIZE, (h + 1) * P_SIZE)
        ybase[:, lanes] = dot(mixing.astype(bf16), conv[:, lanes], ((1,), (0,)))

    diagonal(0)
    diagonal(1)

    def head_decay(ref, heads=4):
        return jnp.concatenate(
            [jnp.broadcast_to(ref[pl.ds(4 * C + i, 1), :], (P_SIZE, N)) for i in range(heads)], axis=0
        )

    a_copy.wait()
    first_core = (C == 0).astype(f32)
    own_half = state[own_rows, :]
    sib_half = sibstate[...].astype(f32)
    own_decay = head_decay(dec.at[0])
    sib_decay = head_decay(dec.at[1])
    total[...] = (
        own_half * (first_core * sib_decay + (1.0 - first_core))
        + sib_half * (first_core + (1.0 - first_core) * own_decay)
    ).astype(bf16)
    b_copies = []
    for k in range(1, NY):
        target = lax.rem(Y + k, NY)
        piece = pl.ds(pl.multiple_of(target * 32, 32), 32)
        copy = remote(total.at[piece], gath.at[Y], scan_send.at[9 + k], scan_recv.at[4], y_at(k))
        copy.start()
        b_copies.append(copy)
    gath[Y] = total[pl.ds(pl.multiple_of(Y * 32, 32), 32), :]

    for h in range(2, 8):
        diagonal(h)

    for copy in dec_copies + b_copies:
        copy.wait_send()
    arrived(decall.at[pl.ds(0, 7)], scan_recv.at[2])
    arrived(gath.at[pl.ds(0, 7)], scan_recv.at[4])
    my_head = 4 * C + Y // 2
    carried = jnp.zeros((32, N), f32)
    for k in range(NY):
        entout[k] = carried.astype(bf16)
        carried = decall[k, pl.ds(my_head, 1), :] * carried + gath[k].astype(f32)
    my_piece = pl.ds(pl.multiple_of(Y * 32, 32), 32)
    c_copies = []
    for k in range(1, NY):
        target = lax.rem(Y + k, NY)
        copy = remote(entout.at[target], entchip.at[my_piece], scan_send.at[16 + k], scan_recv.at[5], y_at(k))
        copy.start()
        c_copies.append(copy)
    entchip[my_piece, :] = entout[Y]

    skip = dot(dsk_ref[...], spread, ((1,), (0,)), HI)
    ybase[...] = ybase[...] + skip * x_conv
    grow = dot(jnp.exp(cum_cols), spread, ((1,), (0,)), HI)
    z_load.wait()

    for copy in c_copies:
        copy.wait_send()
    arrived(entchip.at[pl.ds(0, 224)], scan_recv.at[5])
    enter_first = entchip[...].astype(f32)
    enter_second = enter_first * (first_core * own_decay + (1.0 - first_core) * sib_decay) + (
        first_core * own_half + (1.0 - first_core) * sib_half
    )
    entsend[...] = (first_core * enter_second + (1.0 - first_core) * enter_first).astype(bf16)
    d_copy = remote(entsend, ent.at[own_rows], scan_send.at[24], scan_recv.at[6], sibling)
    d_copy.start()
    ent[own_rows, :] = (first_core * enter_first + (1.0 - first_core) * enter_second).astype(bf16)
    d_copy.wait()

    y_off = dot(c_conv, ent[...], ((1,), (1,)))
    zf = zb[...].astype(f32)
    gated = (ybase[...] + y_off * grow) * (zf / (1.0 + jnp.exp(-zf)))
    sq[0] = dot(jnp.ones((8, CH), f32), gated * gated, ((1,), (1,)), HI)
    in_group = lax.rem(Z, 4)
    sq_copies = []
    for k in range(1, 4):
        target = at(Y, C, X, Z - in_group + lax.rem(in_group + k, 4))
        copy = remote(sq.at[0], sq.at[k], scan_send.at[24 + k], scan_recv.at[6 + k], target)
        copy.start()
        sq_copies.append(copy)
    for copy in sq_copies:
        copy.wait()
    squares = sq[0] + sq[1] + sq[2] + sq[3]
    inv = lax.rsqrt(squares * (1.0 / 2048.0) + norm_eps)
    inv_cols = dot(inv, jnp.full((8, 128), 0.125, f32), ((0,), (0,)), HI)
    scale = jnp.concatenate([inv_cols] * 4, axis=1)
    own_tok = pl.ds(pl.multiple_of(C * TOK, TOK), TOK)
    slot_in[0, own_tok, :] = (gated * scale * gain_ref[...]).astype(bf16)

    def share_rows(side):
        return pl.ds(pl.multiple_of(C * 256 + side * 128, 128), 128)

    def sib_slot_rows(side):
        return pl.ds(pl.multiple_of(other * 256 + side * 128, 128), 128)

    right, left = y_at(1), y_at(NY - 1)

    def share(slot, side):
        return remote(
            slot_in.at[slot, share_rows(side)],
            slot_in.at[slot, share_rows(side)],
            c_send.at[slot, side],
            c_recv.at[slot, side],
            sibling,
        )

    def pass_on(slot, side, src_slot, src_side):
        return remote(
            slot_in.at[src_slot, share_rows(src_side)],
            slot_in.at[slot, share_rows(side)],
            y_send.at[slot, side],
            y_recv.at[slot, side],
            right if side == 0 else left,
        )

    for h in range(2):
        for side in range(2):
            pass_on(1 + h, side, 0, h).start()
        share(0, h).start()
    w_load.wait()

    def x_block(x):
        return pl.ds(pl.multiple_of(lax.rem(x + 2 * NX, NX) * 128, 128), 128)

    def x_long(slot, stage):
        src = part.at[slot, x_block(X + 2 * sigma)] if stage == 0 else xlong.at[slot, 0]
        return remote(src, xlong.at[slot, stage], x_send.at[slot, stage], x_recv.at[slot, stage], x_fwd)

    def x_short(slot):
        return remote(
            part.at[slot, x_block(X - sigma)], xshort.at[slot], x_send.at[slot, 2], x_recv.at[slot, 2], x_back
        )

    def z_copy(slot, k):
        target = lax.rem(Z + k, NZ)
        src = strip.at[slot, pl.ds(pl.multiple_of(target * 16, 16), 16)]
        return remote(src, zin.at[slot, k], z_send.at[slot, k], z_recv.at[slot, k], z_at(k))

    def final_rows(slot):
        half = lax.rem(slot + 1, 2)
        half = jnp.where(jnp.logical_or(slot == 0, slot == 7), lax.rem(X, 2), half)
        return pl.ds(pl.multiple_of(half * 128 + Z * 16, 16), 16)

    def final_y(slot):
        distance = (slot + 1) // 2
        return lax.rem(Y + NY + jnp.where(lax.rem(X, 2) == 0, -distance, distance), NY)

    def final_copy(slot, par):
        return remote(
            fin.at[slot, :, pl.ds(par * 256, 256)],
            out.at[final_rows(slot)],
            f_send.at[slot, par],
            f_recv.at[0],
            at(final_y(slot), owner_c, owner_x, owner_z + par),
        )

    def final_here(slot, par):
        return same(at(final_y(slot), owner_c, owner_x, owner_z + par), me)

    def step_of(t, carry):
        slot = t

        @pl.when(jnp.logical_and(t >= 1, t < SLOTS))
        def _():
            for side in range(2):
                pass_on(slot, side, slot, side).wait_recv()
                share(slot, side).start()

            @pl.when(t <= 4)
            def _():
                for side in range(2):
                    pass_on(slot + 2, side, slot, side).start()

            @pl.when(t == 5)
            def _():
                pass_on(7, 0, slot, 0).start()

            @pl.when(t == 6)
            def _():
                pass_on(7, 1, slot, 1).start()

        s1 = t - 1

        @pl.when(jnp.logical_and(t >= 1, t < SLOTS + 1))
        def _():
            x_long(s1, 0).wait_recv()
            xlong[s1, 0] = (
                xlong[s1, 0].astype(f32) + part[s1, x_block(X + sigma), :].astype(f32)
            ).astype(bf16)
            x_long(s1, 1).start()

        @pl.when(t < SLOTS)
        def _():
            for side in range(2):
                share(slot, side).wait_recv()
            part[slot] = dot(slot_in[slot], wb[...], ((1,), (0,))).astype(bf16)
            x_long(slot, 0).start()
            x_short(slot).start()

        s2 = t - 2

        @pl.when(jnp.logical_and(t >= 2, t < SLOTS + 2))
        def _():
            x_long(s2, 1).wait_recv()
            x_short(s2).wait_recv()
            strip[s2] = (
                xlong[s2, 1].astype(f32) + xshort[s2].astype(f32) + part[s2, x_block(X), :].astype(f32)
            ).astype(bf16)
            for k in range(1, NZ):
                z_copy(s2, k).start()

        s3 = t - 3

        @pl.when(t >= 3)
        def _():
            acc = strip[s3, pl.ds(pl.multiple_of(Z * 16, 16), 16), :].astype(f32)
            for k in range(1, NZ):
                z_copy(s3, k).wait_recv()
                acc = acc + zin[s3, k].astype(f32)
            fin[s3] = acc.astype(bf16)
            for par in range(2):
                here = final_here(s3, par)

                @pl.when(here)
                def _():
                    out[final_rows(s3), :] = fin[s3, :, par * 256 : (par + 1) * 256]

                @pl.when(jnp.logical_not(here))
                def _():
                    final_copy(s3, par).start()

        return carry

    lax.fori_loop(0, SLOTS + 3, step_of, 0)

    def drain(slot, carry):
        @pl.when(slot >= 1)
        def _():
            @pl.when(slot < 7)
            def _():
                for side in range(2):
                    pass_on(slot, side, slot, side).wait_send()

            @pl.when(slot == 7)
            def _():
                for side in range(2):
                    pass_on(7, side, 7, side).wait_send()

        for side in range(2):
            share(slot, side).wait_send()
        x_long(slot, 0).wait_send()
        x_long(slot, 1).wait_send()
        x_short(slot).wait_send()
        for k in range(1, NZ):
            z_copy(slot, k).wait_send()
        for par in range(2):

            @pl.when(jnp.logical_not(final_here(slot, par)))
            def _():
                final_copy(slot, par).wait_send()

        return carry

    lax.fori_loop(0, SLOTS, drain, 0)

    @pl.when(stays == 0)
    def _():
        arrived(out, f_recv.at[0])

    @pl.when(stays == 1)
    def _():
        arrived(out.at[pl.ds(0, TOK - 16)], f_recv.at[0])

    o_ref[...] = out[...]


def per_device(
    x_raw,
    bc_raw,
    z_raw,
    x_kernel,
    bc_kernel,
    x_offset,
    bc_offset,
    dt_raw,
    dt_bias,
    a_log,
    d_skip,
    norm_gain,
    out_weight,
):
    vmem = pl.BlockSpec(memory_space=pltpu.VMEM)
    hbm = pl.BlockSpec(memory_space=pl.ANY)
    V = pltpu.VMEM
    S = pltpu.SemaphoreType.DMA
    return pl.pallas_call(
        kernel,
        out_shape=jax.ShapeDtypeStruct((TOK, 256), bf16),
        in_specs=[hbm, hbm, hbm] + [vmem] * 9 + [hbm],
        out_specs=vmem,
        scratch_shapes=[
            V((TOK, 1024), bf16),
            V((TOK, CH), bf16),
            V((CH, CH), bf16),
            S((5,)),
            V((16, 1024), bf16),
            V((TOK + 8, 1024), f32),
            V((TOK, 1024), bf16),
            V((TOK, 8), f32),
            V((TOK, 8), f32),
            V((16, TOK), f32),
            V((TOK, CH), f32),
            V((CH, N), f32),
            V((CH, N), bf16),
            V((256, N), bf16),
            V((3, 8, 256), f32),
            V((8, 8, 256), f32),
            V((256, N), bf16),
            V((8, 32, N), bf16),
            V((8, 32, N), bf16),
            V((256, N), bf16),
            V((256, N), bf16),
            V((CH, N), bf16),
            V((4, 8, 256), f32),
            V((SLOTS, CH, CH), bf16),
            V((SLOTS, CH, CH), bf16),
            V((SLOTS, 2, 128, CH), bf16),
            V((SLOTS, 128, CH), bf16),
            V((SLOTS, 128, CH), bf16),
            V((SLOTS, 8, 16, CH), bf16),
            V((SLOTS, 16, CH), bf16),
            V((TOK, 256), bf16),
            S((28,)),
            S((10,)),
            S((SLOTS, 2)),
            S((SLOTS, 2)),
            S((SLOTS, 2)),
            S((SLOTS, 2)),
            S((SLOTS, 3)),
            S((SLOTS, 3)),
            S((SLOTS, 8)),
            S((SLOTS, 8)),
            S((SLOTS, 2)),
            S((1,)),
        ],
        compiler_params=pltpu.CompilerParams(
            collective_id=0, has_side_effects=True, vmem_limit_bytes=48 * 1024 * 1024
        ),
        name="mixer",
    )(
        x_raw,
        bc_raw,
        z_raw,
        x_kernel,
        bc_kernel,
        x_offset.reshape(1, -1),
        bc_offset.reshape(1, -1),
        dt_raw,
        dt_bias.reshape(1, -1),
        a_log.reshape(1, -1),
        d_skip.reshape(1, -1),
        norm_gain.reshape(1, -1),
        out_weight,
    )


def solution(mesh):
    return jax.shard_map(
        per_device,
        mesh=mesh,
        in_specs=(
            P("seq", "head"),
            P("seq", None),
            P("seq", "head"),
            P(None, "head"),
            P(),
            P("head"),
            P(),
            P("seq", "head"),
            P("head"),
            P("head"),
            P("head"),
            P("head"),
            P("head", "seq"),
        ),
        out_specs=P("seq", "head"),
        check_vma=False,
    )
```

time: 445 us -> 123 us (0.28)
  the two profiles are of different devices: /device:TPU:8 before, /device:TPU:22 now
where the time goes in v1:
time: 123 us; the launch traced here: 122 us
  Pallas kernels  110 us (89%)
  local copies, waits for them, and re-layouts  11.6 us (9%)
    pallas_call x1, Pallas kernels, per_device(): pl.pallas_call(kernel, out_shape=jax.ShapeDtypeStruct((TOK, 256), bf16),...  110 us
    unnamed x26, local copies, waits for them, and re-layouts  11.6 us

profile of v1, /device:TPU:22, one launch (start us, length us, event | category | flops | bytes accessed | tf_op | source)
XLA Modules:
  0.0 122.0 jit_solution(18291310123897106530)
XLA Ops:
  0.0 0.8 copy.14.dt_ref
  0.8 0.0 copy-start
  0.8 1.6 %copy-done = bf16[256,4096]{1,0:T(8,128)(2,1)S(1)} copy-done((bf16[256,4096]{1,0:T(8,128)(2,1)S(1)}, bf16[256,4096]{1,0:T(8,128)(2,1)}, u32[]{:S(2)}) %copy-start) | copy-done | bytes 2097176
  2.4 0.0 copy-start.1
  2.4 1.0 copy-done.1
  3.5 0.0 copy-start.2
  3.5 0.9 copy-done.2
  4.4 0.0 copy-start.3
  4.4 0.9 copy-done.3
  5.4 0.0 copy-start.4
  5.4 0.8 copy-done.4
  6.2 0.0 copy-start.5
  6.2 0.7 copy-done.5
  6.9 0.0 copy-start.6
  6.9 0.7 copy-done.6
  7.6 0.0 copy-start.7
  7.6 0.7 copy-done.7
  8.3 0.0 copy-start.8
  8.3 0.7 copy-done.8
  9.0 0.0 copy-start.9
  9.0 0.7 copy-done.9
  9.6 0.0 copy-start.10
  9.6 0.7 copy-done.10
  10.3 0.0 copy-start.11
  10.3 0.7 copy-done.11
  11.0 110.4 %mixer.1 = bf16[256,256]{1,0:T(8,128)(2,1)S(1)} custom-call(bf16[256,512]{1,0:T(8,128)(2,1)S(1)} %copy-done.2, bf16[256,4096]{1,0:T(8,128)(2,1)S(1)} %copy-done, bf16[256,512]{1,0:T(8,128)(2,1)S(1)} %copy-done.3, f32[4,512]{1,0:T(4,128)S(1)} %copy-done.6, f32[4,4096]{1,0:T(4,128)S(1)} %copy-done.4, f32[1,512]{1,0:T(1,128)S(1)} %bitcast.7, ...), custom_call_target="tpu_custom_call" | custom-call | tf_op jit(solution)/shard_map/mixer/pallas_call | solution.py:546
  121.4 0.7 copy.16
Async XLA Ops:
  0.8 1.6 %copy-start = (bf16[256,4096]{1,0:T(8,128)(2,1)S(1)}, bf16[256,4096]{1,0:T(8,128)(2,1)}, u32[]{:S(2)}) copy-start(bf16[256,4096]{1,0:T(8,128)(2,1)} %bc_hbm.1) | copy-start | bytes 6291460
  2.4 1.0 copy-start.1
  3.5 0.9 copy-start.2
  4.4 0.9 copy-start.3
  5.4 0.8 copy-start.4
  6.2 0.7 copy-start.5
  6.9 0.7 copy-start.6
  7.6 0.7 copy-start.7
  8.3 0.7 copy-start.8
  9.0 0.7 copy-start.9
  9.6 0.7 copy-start.10
  10.3 0.7 copy-start.11

commit v2 on v1

v2 whole, which is shorter than its diff:
```python
import jax
import jax.numpy as jnp
from jax import lax
from jax.experimental import pallas as pl
from jax.experimental.pallas import tpu as pltpu
from jax.sharding import PartitionSpec as P

P_SIZE = 64
N = 256
TOK = 256
CH = 512
HEADS_DEV = 8
NY, NX, NZ = 8, 4, 8
SLOTS = 8
RING_SLOTS = 4
RING_COLS = 256
LAG_LONG, LAG_STRIP, LAG_FINAL = 2, 4, 6
LAG_RING, LAG_RING_FINAL = 2, 10
STEPS = max(SLOTS + LAG_FINAL, RING_SLOTS + LAG_RING_FINAL)
norm_eps = 1e-05
MESH = pl.DeviceIdType.MESH
HI = lax.Precision.HIGHEST
f32 = jnp.float32
bf16 = jnp.bfloat16


def dot(a, b, dims, precision=None):
    return lax.dot_general(a, b, (dims, ((), ())), precision=precision, preferred_element_type=f32)


def kernel(
    x_hbm,
    bc_hbm,
    z_hbm,
    xk_hbm,
    bck_hbm,
    xo_hbm,
    bco_hbm,
    dt_hbm,
    dtb_hbm,
    alog_hbm,
    dsk_hbm,
    gain_hbm,
    w_hbm,
    o_ref,
    xbc,
    zb,
    wb,
    taps_ref,
    offsets,
    dt_ref,
    dtb_ref,
    alog_ref,
    dsk_ref,
    gain_ref,
    load_sem,
    halo,
    raw,
    conv,
    cum,
    rows,
    ybase,
    gate,
    state,
    statebf,
    sibstate,
    dec,
    decall,
    total,
    gath,
    entout,
    entchip,
    entsend,
    ent,
    sq,
    scales,
    slot_in,
    part,
    xin,
    strip,
    zin,
    fin,
    rlong,
    rshort,
    rstrip,
    rin,
    rfin,
    unused,
    out,
    scan_send,
    scan_recv,
    y_send,
    y_recv,
    x_send,
    x_recv,
    z_send,
    z_recv,
    r_send,
    r_recv,
    f_send,
    f_recv,
):
    seq = lax.axis_index("seq")
    head = lax.axis_index("head")
    Y, C = seq // 2, seq % 2
    X, Z = head // NZ, head % NZ
    group = head // 4
    other = 1 - C

    def at(y, c, x, z):
        return (y * 2 + c, x * NZ + z)

    b_start = pl.multiple_of(group * N, N)
    c_start = pl.multiple_of(8 * N + group * N, N)
    sources = [
        (x_hbm, xbc.at[:, pl.ds(0, CH)]),
        (bc_hbm.at[:, pl.ds(b_start, N)], xbc.at[:, pl.ds(CH, N)]),
        (bc_hbm.at[:, pl.ds(c_start, N)], xbc.at[:, pl.ds(CH + N, N)]),
        (dt_hbm, dt_ref),
        (dtb_hbm, dtb_ref),
        (alog_hbm, alog_ref),
        (xk_hbm, taps_ref.at[:, pl.ds(0, CH)]),
        (bck_hbm.at[:, pl.ds(b_start, N)], taps_ref.at[:, pl.ds(CH, N)]),
        (bck_hbm.at[:, pl.ds(c_start, N)], taps_ref.at[:, pl.ds(CH + N, N)]),
        (xo_hbm, offsets.at[:, pl.ds(0, CH)]),
        (bco_hbm.at[:, pl.ds(b_start, N)], offsets.at[:, pl.ds(CH, N)]),
        (bco_hbm.at[:, pl.ds(c_start, N)], offsets.at[:, pl.ds(CH + N, N)]),
        (dsk_hbm, dsk_ref),
        (gain_hbm, gain_ref),
        (z_hbm, zb),
        (w_hbm, wb.at[C]),
    ]
    loads = [pltpu.make_async_copy(src, dst, load_sem.at[i]) for i, (src, dst) in enumerate(sources)]
    for copy in loads:
        copy.start()

    sibling = at(Y, other, X, Z)
    after = (lax.rem(seq + 1, 16), head)
    cross = at(lax.rem(Y + NY - 1 + 2 * C, NY), other, X, Z)
    sigma = 1 - 2 * C
    x_fwd = at(Y, C, lax.rem(X + NX + sigma, NX), Z)
    x_back = at(Y, C, lax.rem(X + NX - sigma, NX), Z)

    def y_at(k):
        return at(lax.rem(Y + k, NY), C, X, Z)

    def x_at(k):
        return at(Y, C, lax.rem(X + k, NX), Z)

    def z_at(k):
        return at(Y, C, X, lax.rem(Z + k, NZ))

    owner_x = Y // 2
    owner_z = 4 * lax.rem(Y, 2)

    def same(a, b):
        return jnp.logical_and(a[0] == b[0], a[1] == b[1])

    me = (seq, head)

    barrier = pltpu.get_barrier_semaphore()

    def greet(device):
        pl.semaphore_signal(barrier, inc=1, device_id=device, device_id_type=MESH)

    greet(cross)
    greet(sibling)
    for k in range(1, NY):
        greet(y_at(k))
    for k in range(1, NZ):
        greet(z_at(k))
    for k in range(1, NX):
        greet(x_at(k))

    src_y = 2 * X + Z // 4
    src_half = lax.rem(Z // 2, 2)

    def greet_other(device):
        @pl.when(jnp.logical_not(same(device, me)))
        def _():
            greet(device)

    def greet_source(i, carry):
        greet_other(at(src_y, C, 2 * src_half + i // NZ, lax.rem(i, NZ)))
        return carry

    lax.fori_loop(0, 16, greet_source, 0)

    @pl.when(lax.rem(Z, 2) == 1)
    def _():
        def greet_ring_source(i, carry):
            greet_other(at(src_y, C, i // 4, 4 * src_half + lax.rem(i, 4)))
            return carry

        lax.fori_loop(0, 16, greet_ring_source, 0)

    stays = jnp.logical_and(owner_x == X, Z // 2 == (owner_z + 2 * (X // 2)) // 2)
    stays_ring = jnp.logical_and(owner_x == X, Z == owner_z + 2 * (Z // 4) + 1)
    greetings = 2 + (NY - 1) + (NZ - 1) + (NX - 1) + 24
    greetings = greetings - stays.astype(jnp.int32) - stays_ring.astype(jnp.int32)

    pos_t = lax.broadcasted_iota(jnp.int32, (TOK, TOK), 0)
    pos_s = lax.broadcasted_iota(jnp.int32, (TOK, TOK), 1)
    causal = pos_t >= pos_s
    eye = (pos_t == pos_s).astype(f32)
    eye8 = (
        lax.broadcasted_iota(jnp.int32, (8, 8), 0) == lax.broadcasted_iota(jnp.int32, (8, 8), 1)
    ).astype(f32)
    for copy in loads[3:6]:
        copy.wait()
    step_in = dot(dt_ref[...], eye8, ((0,), (0,)), HI) + dtb_ref[...]
    step = jnp.maximum(step_in, 0.0) + jnp.log1p(jnp.exp(-jnp.abs(step_in)))
    log_step = step * -jnp.exp(alog_ref[...])
    cum_cols = dot(causal.astype(f32), log_step, ((1,), (0,)), HI)
    cum[...] = cum_cols
    rows[0:8, :] = dot(cum_cols, eye, ((0,), (0,)), HI)
    rows[8:16, :] = dot(step, eye, ((0,), (0,)), HI)
    last_cols = cum_cols[TOK - 1 : TOK, :]
    dec[0] = jnp.broadcast_to(jnp.exp(rows[0:8, TOK - 1 : TOK]), (8, TOK))
    spread = (
        lax.broadcasted_iota(jnp.int32, (HEADS_DEV, CH), 1) // P_SIZE
        == lax.broadcasted_iota(jnp.int32, (HEADS_DEV, CH), 0)
    ).astype(f32)
    end_weight = dot(jnp.exp(last_cols - cum_cols) * step, spread, ((1,), (0,)), HI)

    for copy in loads[0:3] + loads[6:14]:
        copy.wait()
    raw[8 : 8 + TOK, :] = xbc[...].astype(f32)
    pl.semaphore_wait(barrier, greetings)

    def remote(src, dst, send, recv, device):
        return pltpu.make_async_remote_copy(
            src_ref=src, dst_ref=dst, send_sem=send, recv_sem=recv, device_id=device, device_id_type=MESH
        )

    def arrived(ref, sem):
        pltpu.make_async_copy(ref, ref, sem).wait()

    halo_copy = remote(xbc.at[pl.ds(TOK - 16, 16)], halo, scan_send.at[0], scan_recv.at[0], after)
    halo_copy.start()
    dec_copy = remote(dec.at[0], dec.at[1], scan_send.at[1], scan_recv.at[1], sibling)
    dec_copy.start()

    def convolve(first, count):
        for j in range(8):
            cols = slice(j * 128, (j + 1) * 128)
            acc = jnp.broadcast_to(offsets[:, cols], (count, 128))
            for k in range(4):
                acc = acc + taps_ref[k : k + 1, cols] * raw[5 + k + first : 5 + k + first + count, cols]
            conv[first : first + count, cols] = (acc / (1.0 + jnp.exp(-acc))).astype(bf16)

    convolve(16, TOK - 16)
    halo_copy.wait()
    not_first = (seq > 0).astype(f32)
    raw[0:8, :] = halo[...].astype(f32)[8:16, :] * not_first
    convolve(0, 16)

    x_conv = conv[:, 0:CH].astype(f32)
    weighted = (x_conv * end_weight).astype(bf16)
    own_state = dot(weighted, conv[:, CH : CH + N], ((0,), (0,)))
    state[...] = own_state
    statebf[...] = own_state.astype(bf16)
    sib_rows = pl.ds(pl.multiple_of(other * 256, 256), 256)
    own_rows = pl.ds(pl.multiple_of(C * 256, 256), 256)
    a_copy = remote(statebf.at[sib_rows], sibstate, scan_send.at[4], scan_recv.at[3], sibling)
    a_copy.start()

    dec_copy.wait()
    dec[2] = dec[0] * dec[1]
    for k in range(1, NY):
        remote(dec.at[2], decall.at[Y], scan_send.at[2], scan_recv.at[2], y_at(k)).start()
    decall[Y] = dec[2]

    b_conv = conv[:, CH : CH + N]
    c_conv = conv[:, CH + N : CH + 2 * N]
    inner = dot(c_conv, b_conv, ((1,), (1,)))

    def diagonal(h):
        gap = cum[:, h : h + 1] - rows[h : h + 1, :]
        mixing = jnp.exp(jnp.where(causal, gap, -jnp.inf)) * inner * rows[8 + h : 9 + h, :]
        lanes = slice(h * P_SIZE, (h + 1) * P_SIZE)
        ybase[:, lanes] = dot(mixing.astype(bf16), conv[:, lanes], ((1,), (0,)))

    def head_decay(ref):
        return jnp.concatenate(
            [jnp.broadcast_to(ref[pl.ds(4 * C + i, 1), :], (P_SIZE, N)) for i in range(4)], axis=0
        )

    first_core = (C == 0).astype(f32)
    a_copy.wait()
    total[...] = (
        state[own_rows, :] * (first_core * head_decay(dec.at[1]) + (1.0 - first_core))
        + sibstate[...].astype(f32) * (first_core + (1.0 - first_core) * head_decay(dec.at[0]))
    ).astype(bf16)
    for k in (4, 3, 5, 2, 6, 1, 7):
        target = lax.rem(Y + k, NY)
        piece = pl.ds(pl.multiple_of(target * 32, 32), 32)
        remote(total.at[piece], gath.at[Y], scan_send.at[3], scan_recv.at[4], y_at(k)).start()
    gath[Y] = total[pl.ds(pl.multiple_of(Y * 32, 32), 32), :]

    loads[15].wait()
    w_copy = remote(wb.at[C], wb.at[C], scan_send.at[8], scan_recv.at[8], sibling)
    w_copy.start()

    for h in range(8):
        diagonal(h)

    arrived(decall.at[pl.ds(0, 7)], scan_recv.at[2])
    arrived(gath.at[pl.ds(0, 7)], scan_recv.at[4])
    my_head = 4 * C + Y // 2
    carried = jnp.zeros((32, N), f32)
    for k in range(NY):
        entout[k] = carried.astype(bf16)
        carried = decall[k, pl.ds(my_head, 1), :] * carried + gath[k].astype(f32)
    my_piece = pl.ds(pl.multiple_of(Y * 32, 32), 32)
    for k in (4, 3, 5, 2, 6, 1, 7):
        target = lax.rem(Y + k, NY)
        remote(entout.at[target], entchip.at[my_piece], scan_send.at[5], scan_recv.at[5], y_at(k)).start()
    entchip[my_piece, :] = entout[Y]

    skip = dot(dsk_ref[...], spread, ((1,), (0,)), HI)
    loads[14].wait()
    zf = zb[...].astype(f32)
    silu_z = zf / (1.0 + jnp.exp(-zf))
    ybase[...] = (ybase[...] + skip * conv[:, 0:CH].astype(f32)) * silu_z
    gate[...] = silu_z * dot(jnp.exp(cum_cols), spread, ((1,), (0,)), HI)

    arrived(entchip.at[pl.ds(0, 224)], scan_recv.at[5])
    enter_first = entchip[...].astype(f32)
    enter_second = enter_first * (
        first_core * head_decay(dec.at[0]) + (1.0 - first_core) * head_decay(dec.at[1])
    ) + (first_core * state[own_rows, :] + (1.0 - first_core) * sibstate[...].astype(f32))
    entsend[...] = (first_core * enter_second + (1.0 - first_core) * enter_first).astype(bf16)
    d_copy = remote(entsend, ent.at[own_rows], scan_send.at[6], scan_recv.at[6], sibling)
    d_copy.start()
    ent[own_rows, :] = (first_core * enter_first + (1.0 - first_core) * enter_second).astype(bf16)
    d_copy.wait()

    y_off = dot(conv[:, CH + N : CH + 2 * N], ent[...], ((1,), (1,)))
    gated = ybase[...] + y_off * gate[...]
    slot_in[0] = (gated * gain_ref[...]).astype(bf16)

    def half_rows(side):
        return pl.ds(side * 128, 128)

    right, left = y_at(1), y_at(NY - 1)

    def pass_on(slot, side, src_slot, src_side):
        return remote(
            slot_in.at[src_slot, half_rows(src_side)],
            slot_in.at[slot, half_rows(side)],
            y_send.at[side],
            y_recv.at[slot, side],
            right if side == 0 else left,
        )

    for h in range(2):
        for side in range(2):
            pass_on(1 + h, side, 0, h).start()

    sq[0] = dot(jnp.ones((8, CH), f32), gated * gated, ((1,), (1,)), HI)
    in_group = lax.rem(Z, 4)
    for k in (3, 2, 1):
        target = at(Y, C, X, Z - in_group + lax.rem(in_group + k, 4))
        remote(sq.at[0], sq.at[k], scan_send.at[7], scan_recv.at[7], target).start()
    w_copy.wait()
    arrived(decall.at[pl.ds(0, 7)], scan_send.at[2])
    arrived(gath.at[pl.ds(0, 7)], scan_send.at[3])
    arrived(entchip.at[pl.ds(0, 224)], scan_send.at[5])
    arrived(sq.at[pl.ds(0, 3)], scan_recv.at[7])
    squares = sq[0] + sq[1] + sq[2] + sq[3]
    scales[Y] = lax.rsqrt(squares * (1.0 / 2048.0) + norm_eps)[0:1, :]
    for k in (4, 3, 5, 2, 6, 1, 7):
        remote(scales.at[Y], scales.at[Y], scan_send.at[9], scan_recv.at[9], y_at(k)).start()

    def scale_columns(slot, side):
        k = (slot + 1) // 2
        half = side if slot in (0, 7) else (slot + 1) % 2
        block = lax.rem(Y + NY + (k if side else -k), NY)
        row = jnp.broadcast_to(scales[block, :, half * 128 : half * 128 + 128], (8, 128))
        column = dot(row, jnp.full((8, 128), 0.125, f32), ((0,), (0,)), HI)
        return jnp.concatenate([column] * 4, axis=1)

    def width(slot):
        return pl.ds(0, CH - RING_COLS if slot < RING_SLOTS else CH)

    def x_block(x):
        return lax.rem(x + 2 * NX, NX)

    def x_long(slot, stage):
        cols = width(slot)
        src = part.at[slot, x_block(X + 2 * sigma), :, cols] if stage == 0 else xin.at[slot, 0, :, cols]
        return remote(src, xin.at[slot, stage, :, cols], x_send.at[slot], x_recv.at[slot, stage], x_fwd)

    def x_short(slot):
        cols = width(slot)
        return remote(
            part.at[slot, x_block(X - sigma), :, cols],
            xin.at[slot, 2, :, cols],
            x_send.at[slot],
            x_recv.at[slot, 1],
            x_back,
        )

    def z_copy(slot, k):
        target = lax.rem(Z + k, NZ)
        src = strip.at[slot, pl.ds(pl.multiple_of(target * 16, 16), 16), width(slot)]
        return remote(src, zin.at[slot, k - 1, :, width(slot)], z_send.at[slot], z_recv.at[slot], z_at(k))

    tail = pl.ds(CH - RING_COLS, RING_COLS)
    z_fwd, z_back = z_at(NZ + sigma), z_at(NZ - sigma)

    def z_block(slot, z):
        z = lax.rem(z + 2 * NZ, NZ)
        return part.at[slot, z // 2, pl.ds(pl.multiple_of(lax.rem(z, 2) * 64, 64), 64), tail]

    def ring_long(slot, stage):
        src = z_block(slot, Z + 4 * sigma) if stage == 0 else rlong.at[slot, stage - 1]
        return remote(src, rlong.at[slot, stage], r_send.at[slot, 0], r_recv.at[slot, stage], z_fwd)

    def ring_short(slot, stage):
        src = z_block(slot, Z - 3 * sigma) if stage == 0 else rshort.at[slot, stage - 1]
        return remote(src, rshort.at[slot, stage], r_send.at[slot, 1], r_recv.at[slot, 4 + stage], z_back)

    def ring_x(slot, k):
        target = lax.rem(X + k, NX)
        src = rstrip.at[slot, pl.ds(pl.multiple_of(target * 16, 16), 16)]
        return remote(src, rin.at[slot, k - 1], r_send.at[slot, 2], r_recv.at[slot, 7], x_at(k))

    def strip_row(slot, half, offset):
        if slot not in (0, 7):
            half = 1 - slot % 2
        return pl.ds(pl.multiple_of(half * 128 + offset, 16), 16)

    def strip_y(slot, side):
        distance = (slot + 1) // 2
        return lax.rem(Y + NY + jnp.where(side == 0, -distance, distance), NY)

    def hand_over(src, rows_to, cols_to, device):
        here = same(device, me)
        dst = out.at[rows_to, cols_to]

        @pl.when(here)
        def _():
            pltpu.make_async_copy(src, dst, f_recv.at[0]).start()
            pltpu.make_async_copy(src, unused.at[:, cols_to], f_send.at[0]).start()

        @pl.when(jnp.logical_not(here))
        def _():
            remote(src, dst, f_send.at[0], f_recv.at[0], device).start()

    def add(*values):
        acc = values[0].astype(f32)
        for value in values[1:]:
            acc = acc + value.astype(f32)
        return acc.astype(bf16)

    for t in range(STEPS):
        if 1 <= t < SLOTS:
            for side in range(2):
                pass_on(t, side, t, side).wait_recv()
                if t <= 4:
                    pass_on(t + 2, side, t, side).start()
                if t == 5 + side:
                    pass_on(7, side, t, side).start()

        if t < SLOTS:
            if t == 1:
                arrived(scales.at[pl.ds(0, 7)], scan_recv.at[9])
            scale = [scale_columns(t, side) for side in range(2)]
            for half in range(2):
                product = dot(slot_in[t], wb[half], ((1,), (0,)))
                for side in range(2):
                    part[t, 2 * half + side] = (product[side * 128 : side * 128 + 128] * scale[side]).astype(bf16)
            x_long(t, 0).start()
            x_short(t).start()
            if t < RING_SLOTS:
                ring_long(t, 0).start()
                ring_short(t, 0).start()

        slot = t - LAG_LONG
        if 0 <= slot < SLOTS:
            cols = width(slot)
            x_long(slot, 0).wait_recv()
            xin[slot, 0, :, cols] = add(xin[slot, 0, :, cols], part[slot, x_block(X + sigma), :, cols])
            x_long(slot, 1).start()

        for stage in range(1, 5):
            slot = t - stage * LAG_RING
            if not 0 <= slot < RING_SLOTS:
                continue
            ring_long(slot, stage - 1).wait_recv()
            if stage < 4:
                ring_short(slot, stage - 1).wait_recv()
                block = z_block(slot, Z + (4 - stage) * sigma)
                rlong[slot, stage - 1] = add(rlong[slot, stage - 1], block[...])
                ring_long(slot, stage).start()
            if stage < 3:
                block = z_block(slot, Z - (3 - stage) * sigma)
                rshort[slot, stage - 1] = add(rshort[slot, stage - 1], block[...])
                ring_short(slot, stage).start()
            if stage == 4:
                rstrip[slot] = add(rlong[slot, 3], rshort[slot, 2], z_block(slot, Z)[...])
                for k in (2, 1, 3):
                    ring_x(slot, k).start()

        slot = t - LAG_STRIP
        if 0 <= slot < SLOTS:
            cols = width(slot)
            arrived(xin.at[slot, pl.ds(1, 2), :, cols], x_recv.at[slot, 1])
            strip[slot, :, cols] = add(
                xin[slot, 1, :, cols], xin[slot, 2, :, cols], part[slot, X, :, cols]
            )
            for k in (4, 3, 5, 2, 6, 1, 7):
                z_copy(slot, k).start()

        slot = t - LAG_FINAL
        if 0 <= slot < SLOTS:
            cols = width(slot)
            arrived(zin.at[slot, :, :, cols], z_recv.at[slot])
            fin[slot, :, cols] = add(
                strip[slot, pl.ds(pl.multiple_of(Z * 16, 16), 16), cols],
                *[zin[slot, k, :, cols] for k in range(NZ - 1)],
            )
            side = lax.rem(X, 2)
            rows_to = strip_row(slot, side, Z * 16)
            y_to = strip_y(slot, side)
            z_to = owner_z + 2 * (X // 2)
            hand_over(fin.at[slot, :, pl.ds(0, 256)], rows_to, pl.ds(0, 256), at(y_to, C, owner_x, z_to))
            count = 256 - RING_COLS if slot < RING_SLOTS else 256
            hand_over(
                fin.at[slot, :, pl.ds(256, count)], rows_to, pl.ds(0, count), at(y_to, C, owner_x, z_to + 1)
            )

        slot = t - LAG_RING_FINAL
        if 0 <= slot < RING_SLOTS:
            arrived(rin.at[slot], r_recv.at[slot, 7])
            rfin[slot] = add(
                rstrip[slot, pl.ds(pl.multiple_of(X * 16, 16), 16), :], *[rin[slot, k] for k in range(NX - 1)]
            )
            side = lax.rem(Z // 2, 2)
            owner = at(strip_y(slot, side), C, owner_x, owner_z + 2 * (Z // 4) + 1)
            rows_to = strip_row(slot, side, lax.rem(Z, 2) * 64 + X * 16)
            hand_over(rfin.at[slot], rows_to, pl.ds(256 - RING_COLS, RING_COLS), owner)

    arrived(sq.at[pl.ds(0, 3)], scan_send.at[7])
    arrived(scales.at[pl.ds(0, 7)], scan_send.at[9])
    for side in range(2):
        arrived(slot_in.at[pl.ds(0, 7), pl.ds(0, 128)], y_send.at[side])
    for slot in range(SLOTS):
        arrived(xin.at[slot, :, :, width(slot)], x_send.at[slot])
        arrived(zin.at[slot, :, :, width(slot)], z_send.at[slot])
    for slot in range(RING_SLOTS):
        arrived(rlong.at[slot], r_send.at[slot, 0])
        arrived(rshort.at[slot], r_send.at[slot, 1])
        arrived(rin.at[slot], r_send.at[slot, 2])
    arrived(out, f_send.at[0])
    arrived(out, f_recv.at[0])

    o_ref[...] = out[...]


def per_device(
    x_raw,
    bc_raw,
    z_raw,
    x_kernel,
    bc_kernel,
    x_offset,
    bc_offset,
    dt_raw,
    dt_bias,
    a_log,
    d_skip,
    norm_gain,
    out_weight,
):
    hbm = pl.BlockSpec(memory_space=pltpu.HBM)
    V = pltpu.VMEM
    S = pltpu.SemaphoreType.DMA
    return pl.pallas_call(
        kernel,
        out_shape=jax.ShapeDtypeStruct((TOK, 256), bf16),
        in_specs=[hbm] * 13,
        out_specs=pl.BlockSpec(memory_space=pltpu.VMEM),
        scratch_shapes=[
            V((TOK, 1024), bf16),
            V((TOK, CH), bf16),
            V((2, CH, CH), bf16),
            V((4, 1024), f32),
            V((1, 1024), f32),
            V((8, TOK), f32),
            V((1, 8), f32),
            V((1, 8), f32),
            V((1, 8), f32),
            V((1, CH), f32),
            S((16,)),
            V((16, 1024), bf16),
            V((TOK + 8, 1024), f32),
            V((TOK, 1024), bf16),
            V((TOK, 8), f32),
            V((16, TOK), f32),
            V((TOK, CH), f32),
            V((TOK, CH), f32),
            V((CH, N), f32),
            V((CH, N), bf16),
            V((256, N), bf16),
            V((3, 8, 256), f32),
            V((8, 8, 256), f32),
            V((256, N), bf16),
            V((8, 32, N), bf16),
            V((8, 32, N), bf16),
            V((256, N), bf16),
            V((256, N), bf16),
            V((CH, N), bf16),
            V((4, 8, 256), f32),
            V((NY, 1, TOK), f32),
            V((SLOTS, TOK, CH), bf16),
            V((SLOTS, 4, 128, CH), bf16),
            V((SLOTS, 3, 128, CH), bf16),
            V((SLOTS, 128, CH), bf16),
            V((SLOTS, 7, 16, CH), bf16),
            V((SLOTS, 16, CH), bf16),
            V((RING_SLOTS, 4, 64, RING_COLS), bf16),
            V((RING_SLOTS, 3, 64, RING_COLS), bf16),
            V((RING_SLOTS, 64, RING_COLS), bf16),
            V((RING_SLOTS, 3, 16, RING_COLS), bf16),
            V((RING_SLOTS, 16, RING_COLS), bf16),
            V((16, 256), bf16),
            V((TOK, 256), bf16),
            S((10,)),
            S((10,)),
            S((2,)),
            S((SLOTS, 2)),
            S((SLOTS,)),
            S((SLOTS, 2)),
            S((SLOTS,)),
            S((SLOTS,)),
            S((RING_SLOTS, 3)),
            S((RING_SLOTS, 8)),
            S((1,)),
            S((1,)),
        ],
        compiler_params=pltpu.CompilerParams(
            collective_id=0, has_side_effects=True, vmem_limit_bytes=56 * 1024 * 1024
        ),
        name="mixer",
    )(
        x_raw,
        bc_raw,
        z_raw,
        x_kernel,
        bc_kernel,
        x_offset.reshape(1, -1),
        bc_offset.reshape(1, -1),
        dt_raw.T,
        dt_bias.reshape(1, -1),
        a_log.reshape(1, -1),
        d_skip.reshape(1, -1),
        norm_gain.reshape(1, -1),
        out_weight,
    )


def solution(mesh):
    return jax.shard_map(
        per_device,
        mesh=mesh,
        in_specs=(
            P("seq", "head"),
            P("seq", None),
            P("seq", "head"),
            P(None, "head"),
            P(),
            P("head"),
            P(),
            P("seq", "head"),
            P("head"),
            P("head"),
            P("head"),
            P("head"),
            P("head", "seq"),
        ),
        out_specs=P("seq", "head"),
        check_vma=False,
    )
```

time: 123 us -> 90.5 us (0.74)
  the two profiles are of different devices: /device:TPU:22 before, /device:TPU:4 now
where the time goes in v2:
time: 90.5 us; the launch traced here: 90.3 us
  Pallas kernels  88.8 us (98%)
  local copies, waits for them, and re-layouts  1.57 us (2%)
    pallas_call x1, Pallas kernels, per_device(): pl.pallas_call(kernel, out_shape=jax.ShapeDtypeStruct((TOK, 256), bf16),...  88.8 us

profile of v2, /device:TPU:4, one launch (start us, length us, event | category | flops | bytes accessed | tf_op | source)
XLA Modules:
  0.0 90.3 jit_solution(1880352430103509976)
XLA Ops:
  0.0 88.8 %mixer.1 = bf16[256,256]{1,0:T(8,128)(2,1)} custom-call(bf16[256,512]{1,0:T(8,128)(2,1)} %x_hbm.1, bf16[256,4096]{1,0:T(8,128)(2,1)} %bc_hbm.1, bf16[256,512]{1,0:T(8,128)(2,1)} %z_hbm.1, f32[4,512]{1,0:T(4,128)} %xk_hbm.1, f32[4,4096]{1,0:T(4,128)} %bck_hbm.1, f32[1,512]{1,0:T(1,128)} %bitcast.9, f32[1,4096]{1,0:T(1,128)} %bitcast.7, f32[8,256]{1,0:T(8,128)} %bitcast.8, ...), custom_call_target="tpu_custom_call" | custom-call | tf_op jit(solution)/shard_map/mixer/pallas_call | solution.py:581
  88.8 1.6 %copy.15 = bf16[256,256]{1,0:T(8,128)(2,1)} copy(bf16[256,256]{1,0:T(8,128)(2,1)} %mixer.1) | data formatting | bytes 262144

commit v3 on v2

--- a/solution.py
+++ b/solution.py
@@ -12,7 +12,7 @@
 HEADS_DEV = 8
 NY, NX, NZ = 8, 4, 8
 SLOTS = 8
-RING_SLOTS = 4
+RING_SLOTS = 5
 RING_COLS = 256
 LAG_LONG, LAG_STRIP, LAG_FINAL = 2, 4, 6
 LAG_RING, LAG_RING_FINAL = 2, 10
@@ -226,21 +226,6 @@
     for copy in loads[0:3] + loads[6:14]:
         copy.wait()
     raw[8 : 8 + TOK, :] = xbc[...].astype(f32)
-    pl.semaphore_wait(barrier, greetings)
-
-    def remote(src, dst, send, recv, device):
-        return pltpu.make_async_remote_copy(
-            src_ref=src, dst_ref=dst, send_sem=send, recv_sem=recv, device_id=device, device_id_type=MESH
-        )
-
-    def arrived(ref, sem):
-        pltpu.make_async_copy(ref, ref, sem).wait()
-
-    halo_copy = remote(xbc.at[pl.ds(TOK - 16, 16)], halo, scan_send.at[0], scan_recv.at[0], after)
-    halo_copy.start()
-    dec_copy = remote(dec.at[0], dec.at[1], scan_send.at[1], scan_recv.at[1], sibling)
-    dec_copy.start()
-
     def convolve(first, count):
         for j in range(8):
             cols = slice(j * 128, (j + 1) * 128)
@@ -250,14 +235,34 @@
             conv[first : first + count, cols] = (acc / (1.0 + jnp.exp(-acc))).astype(bf16)
 
     convolve(16, TOK - 16)
+
+    def state_of(first, count):
+        pick = slice(first, first + count)
+        weighted = (conv[pick, 0:CH].astype(f32) * end_weight[pick, :]).astype(bf16)
+        return dot(weighted, conv[pick, CH : CH + N], ((0,), (0,)))
+
+    state[...] = state_of(16, TOK - 16)
+    pl.semaphore_wait(barrier, greetings)
+
+    def remote(src, dst, send, recv, device):
+        return pltpu.make_async_remote_copy(
+            src_ref=src, dst_ref=dst, send_sem=send, recv_sem=recv, device_id=device, device_id_type=MESH
+        )
+
+    def arrived(ref, sem):
+        pltpu.make_async_copy(ref, ref, sem).wait()
+
+    halo_copy = remote(xbc.at[pl.ds(TOK - 16, 16)], halo, scan_send.at[0], scan_recv.at[0], after)
+    halo_copy.start()
+    dec_copy = remote(dec.at[0], dec.at[1], scan_send.at[1], scan_recv.at[1], sibling)
+    dec_copy.start()
+
     halo_copy.wait()
     not_first = (seq > 0).astype(f32)
     raw[0:8, :] = halo[...].astype(f32)[8:16, :] * not_first
     convolve(0, 16)
 
-    x_conv = conv[:, 0:CH].astype(f32)
-    weighted = (x_conv * end_weight).astype(bf16)
-    own_state = dot(weighted, conv[:, CH : CH + N], ((0,), (0,)))
+    own_state = state[...] + state_of(0, 16)
     state[...] = own_state
     statebf[...] = own_state.astype(bf16)
     sib_rows = pl.ds(pl.multiple_of(other * 256, 256), 256)
@@ -358,20 +363,24 @@
         for side in range(2):
             pass_on(1 + h, side, 0, h).start()
 
-    sq[0] = dot(jnp.ones((8, CH), f32), gated * gated, ((1,), (1,)), HI)
+    squared = gated * gated
+    folded = squared[:, 0:128] + squared[:, 128:256] + squared[:, 256:384] + squared[:, 384:512]
+    sq[0] = dot(jnp.ones((8, 128), f32), folded, ((1,), (1,)), HI)
     in_group = lax.rem(Z, 4)
     for k in (3, 2, 1):
         target = at(Y, C, X, Z - in_group + lax.rem(in_group + k, 4))
         remote(sq.at[0], sq.at[k], scan_send.at[7], scan_recv.at[7], target).start()
     w_copy.wait()
+    first_products = [dot(slot_in[0], wb[half], ((1,), (0,))) for half in range(2)]
     arrived(decall.at[pl.ds(0, 7)], scan_send.at[2])
     arrived(gath.at[pl.ds(0, 7)], scan_send.at[3])
     arrived(entchip.at[pl.ds(0, 224)], scan_send.at[5])
     arrived(sq.at[pl.ds(0, 3)], scan_recv.at[7])
     squares = sq[0] + sq[1] + sq[2] + sq[3]
     scales[Y] = lax.rsqrt(squares * (1.0 / 2048.0) + norm_eps)[0:1, :]
-    for k in (4, 3, 5, 2, 6, 1, 7):
-        remote(scales.at[Y], scales.at[Y], scan_send.at[9], scan_recv.at[9], y_at(k)).start()
+    for k in (1, 7, 2, 6, 3, 5, 4):
+        distance = min(k, NY - k)
+        remote(scales.at[Y], scales.at[Y], scan_send.at[9], scan_recv.at[8 + distance], y_at(k)).start()
 
     def scale_columns(slot, side):
         k = (slot + 1) // 2
@@ -465,11 +474,11 @@
                     pass_on(7, side, t, side).start()
 
         if t < SLOTS:
-            if t == 1:
-                arrived(scales.at[pl.ds(0, 7)], scan_recv.at[9])
+            if t % 2 == 1:
+                arrived(scales.at[pl.ds(0, 2 if t < 7 else 1)], scan_recv.at[9 + t // 2])
             scale = [scale_columns(t, side) for side in range(2)]
             for half in range(2):
-                product = dot(slot_in[t], wb[half], ((1,), (0,)))
+                product = first_products[half] if t == 0 else dot(slot_in[t], wb[half], ((1,), (0,)))
                 for side in range(2):
                     part[t, 2 * half + side] = (product[side * 128 : side * 128 + 128] * scale[side]).astype(bf16)
             x_long(t, 0).start()
@@ -629,7 +638,7 @@
             V((16, 256), bf16),
             V((TOK, 256), bf16),
             S((10,)),
-            S((10,)),
+            S((13,)),
             S((2,)),
             S((SLOTS, 2)),
             S((SLOTS,)),

time: 90.5 us -> 88.9 us (0.982)
  Pallas kernels: 88.8 us -> 87.2 us
    pallas_call x1, Pallas kernels: 88.8 us -> 87.2 us  [per_device(): pl.pallas_call(kernel, out_shape=jax.ShapeDtypeStruct((TOK, 256), bf16),...]
where the time goes in v3:
time: 88.9 us; the launch traced here: 88.8 us
  Pallas kernels  87.2 us (98%)
  local copies, waits for them, and re-layouts  1.57 us (2%)
    pallas_call x1, Pallas kernels, per_device(): pl.pallas_call(kernel, out_shape=jax.ShapeDtypeStruct((TOK, 256), bf16),...  87.2 us

profile of v3, /device:TPU:4, one launch (start us, length us, event | category | flops | bytes accessed | tf_op | source)
XLA Modules:
  0.0 88.8 jit_solution(9507752145192821922)
XLA Ops:
  0.0 87.2 %mixer.1 = bf16[256,256]{1,0:T(8,128)(2,1)} custom-call(bf16[256,512]{1,0:T(8,128)(2,1)} %x_hbm.1, bf16[256,4096]{1,0:T(8,128)(2,1)} %bc_hbm.1, bf16[256,512]{1,0:T(8,128)(2,1)} %z_hbm.1, f32[4,512]{1,0:T(4,128)} %xk_hbm.1, f32[4,4096]{1,0:T(4,128)} %bck_hbm.1, f32[1,512]{1,0:T(1,128)} %bitcast.9, f32[1,4096]{1,0:T(1,128)} %bitcast.7, f32[8,256]{1,0:T(8,128)} %bitcast.8, ...), custom_call_target="tpu_custom_call" | custom-call | tf_op jit(solution)/shard_map/mixer/pallas_call | solution.py:590
  87.2 1.6 %copy.15 = bf16[256,256]{1,0:T(8,128)(2,1)} copy(bf16[256,256]{1,0:T(8,128)(2,1)} %mixer.1) | data formatting | bytes 262144

commit v4 on v3

--- a/solution.py
+++ b/solution.py
@@ -163,15 +163,6 @@
     def greet(device):
         pl.semaphore_signal(barrier, inc=1, device_id=device, device_id_type=MESH)
 
-    greet(cross)
-    greet(sibling)
-    for k in range(1, NY):
-        greet(y_at(k))
-    for k in range(1, NZ):
-        greet(z_at(k))
-    for k in range(1, NX):
-        greet(x_at(k))
-
     src_y = 2 * X + Z // 4
     src_half = lax.rem(Z // 2, 2)
 
@@ -193,6 +184,15 @@
             return carry
 
         lax.fori_loop(0, 16, greet_ring_source, 0)
+
+    for k in (4, 3, 5, 2, 6, 1, 7):
+        greet(z_at(k))
+    for k in (4, 3, 5, 2, 6, 1, 7):
+        greet(y_at(k))
+    for k in range(1, NX):
+        greet(x_at(k))
+    greet(cross)
+    greet(sibling)
 
     stays = jnp.logical_and(owner_x == X, Z // 2 == (owner_z + 2 * (X // 2)) // 2)
     stays_ring = jnp.logical_and(owner_x == X, Z == owner_z + 2 * (Z // 4) + 1)

time: 88.9 us -> 87.3 us (0.982)
  Pallas kernels: 87.2 us -> 85.6 us
    pallas_call x1, Pallas kernels: 87.2 us -> 85.6 us  [per_device(): pl.pallas_call(kernel, out_shape=jax.ShapeDtypeStruct((TOK, 256), bf16),...]
where the time goes in v4:
time: 87.3 us; the launch traced here: 87.2 us
  Pallas kernels  85.6 us (98%)
  local copies, waits for them, and re-layouts  1.57 us (2%)
    pallas_call x1, Pallas kernels, per_device(): pl.pallas_call(kernel, out_shape=jax.ShapeDtypeStruct((TOK, 256), bf16),...  85.6 us

profile of v4, /device:TPU:4, one launch (start us, length us, event | category | flops | bytes accessed | tf_op | source)
XLA Modules:
  0.0 87.2 jit_solution(15472226814179519573)
XLA Ops:
  0.0 85.6 %mixer.1 = bf16[256,256]{1,0:T(8,128)(2,1)} custom-call(bf16[256,512]{1,0:T(8,128)(2,1)} %x_hbm.1, bf16[256,4096]{1,0:T(8,128)(2,1)} %bc_hbm.1, bf16[256,512]{1,0:T(8,128)(2,1)} %z_hbm.1, f32[4,512]{1,0:T(4,128)} %xk_hbm.1, f32[4,4096]{1,0:T(4,128)} %bck_hbm.1, f32[1,512]{1,0:T(1,128)} %bitcast.9, f32[1,4096]{1,0:T(1,128)} %bitcast.7, f32[8,256]{1,0:T(8,128)} %bitcast.8, ...), custom_call_target="tpu_custom_call" | custom-call | tf_op jit(solution)/shard_map/mixer/pallas_call | solution.py:590
  85.6 1.6 %copy.15 = bf16[256,256]{1,0:T(8,128)(2,1)} copy(bf16[256,256]{1,0:T(8,128)(2,1)} %mixer.1) | data formatting | bytes 262144
